TPU v7x, 32 devices: a whole 2x2x4 slice. The times are simulated.
32 devices in a mesh: chan: 2 (over y), dp: 16 (over z, x, core).
Axes of the slice: x: 2, y: 2, z: 4, core: 2. Of those that a mesh axis runs over, the one named last changes fastest.
Arguments:
- volume: bfloat16 [32, 32, 32, 256], P('dp', None, None, 'chan'), may hold values from -6 to 6
- filter_one: bfloat16 [3, 3, 3, 256, 256], P(None, None, None, 'chan'), may hold values from -0.078125 to 0.078125
- filter_two: bfloat16 [3, 3, 3, 256, 256], P(None, None, None, 'chan'), may hold values from -0.078125 to 0.078125
- cotangent: bfloat16 [32, 32, 32, 256], P('dp', None, None, 'chan'), may hold values from -6 to 6
Outputs:
- output: bfloat16 [32, 32, 32, 256], P('dp', None, None, 'chan')
- input_grad: bfloat16 [32, 32, 32, 256], P('dp', None, None, 'chan')
- grad_one: float32 [3, 3, 3, 256, 256], P(None, None, None, 'chan')
- grad_two: float32 [3, 3, 3, 256, 256], P(None, None, None, 'chan')
All inputs are finite; a program needn't handle non-finite values.
Results may differ from a plain program's by a relative error of at most 0.02525.
The roundings to bfloat16 on the way count: a program that leaves them out, or rounds other values in their place, can miss the bound.
Values may be sent and summed in bfloat16 or wider, within the bound.
No kernel may reach another device: no remote copies, remote signals or barrier semaphores. Data moves between devices by JAX's collectives and lax.ppermute only.
A program may use at most 128 MiB of HBM per device.

v0:
```python
import functools
import math

import jax
import jax.numpy as jnp
from jax import lax
from jax.experimental import pallas as pl
from jax.experimental.pallas import tpu as pltpu
from jax.sharding import PartitionSpec as P

VOX = 32
SLOPE = 0.3
HALF = 128
FULL = 256
TILE = 16
SMALL = 10**9
VMEM_LIMIT = 32 * 1024 * 1024


def extended(block, sides, width):
    for axis, dim in sides:
        count = lax.axis_size(axis)
        forward = [(i, i + 1) for i in range(count - 1)]
        forward.append((count - 1, 0))
        backward = [(target, source) for source, target in forward]
        low = lax.ppermute(
            lax.slice_in_dim(block, block.shape[dim] - width, None, axis=dim), axis, forward
        )
        high = lax.ppermute(lax.slice_in_dim(block, 0, width, axis=dim), axis, backward)
        block = jnp.concatenate([low, block, high], axis=dim)
    return block


def leaky(values):
    return jnp.where(values > 0, values, SLOPE * values)


def slope_of(values):
    return jnp.where(values > 0, jnp.float32(1.0), jnp.float32(SLOPE))


def tap_mask(rows, offset):
    base = lax.axis_index("dp") * rows
    total_rows = lax.axis_size("dp") * rows
    planes = jnp.mod(base + jnp.arange(rows, dtype=jnp.int32) - 1, total_rows)
    depth = jnp.mod(planes, VOX) + offset
    inside = jnp.logical_and(depth >= 0, depth < VOX)
    return inside[:, None, None, None]


def pad_plane(values):
    return jnp.pad(values, ((0, 0), (1, 1), (1, 1), (0, 0)))


def columns(plane, rows, height, breadth):
    taps = []
    for a in range(3):
        inside = tap_mask(rows, a - 1)
        depth_slab = plane[a : a + rows]
        depth_slab = jnp.where(inside, depth_slab, jnp.zeros_like(depth_slab))
        for b in range(3):
            for c in range(3):
                taps.append(depth_slab[:, b : b + height, c : c + breadth, :])
    stacked = jnp.concatenate(taps, axis=-1)
    return stacked.reshape(rows * height * breadth, stacked.shape[-1])


def plain(volume, filter_one, filter_two, cotangent):
    rows, height, breadth, narrow = volume.shape
    full = filter_one.shape[4]
    voxels = rows * height * breadth
    scale = 1.0 / math.sqrt(lax.axis_size("dp") * voxels)

    def forward(activity, weight):
        rim = extended(activity, (("dp", 0),), 1)
        plane = pad_plane(rim)
        stacked = columns(plane, rows, height, breadth)
        partial_value = jnp.dot(
            stacked, weight.reshape(27 * narrow, full), preferred_element_type=jnp.float32
        )
        summed = lax.psum_scatter(partial_value, "chan", scatter_dimension=1, tiled=True)
        return (plane, summed)

    def backward(plane, delta, weight):
        wide = lax.all_gather(delta, "chan", axis=3, tiled=True)
        rim = extended(wide, (("dp", 0),), 1)
        centre = rim[1 : rows + 1].reshape(voxels, full)
        stacked = columns(plane, rows, height, breadth)
        weight_grad = lax.dot_general(
            stacked, centre, (((0,), (0,)), ((), ())), preferred_element_type=jnp.float32
        )
        weight_grad = weight_grad.reshape(3, 3, 3, narrow, full)
        source = pad_plane(rim)
        total = jnp.zeros((rows, height, breadth, narrow), jnp.float32)
        for a in range(3):
            depth_slab = source[2 - a : 2 - a + rows]
            flat = depth_slab.reshape(-1, full)
            product = lax.dot_general(
                flat,
                weight[a].reshape(9 * narrow, full),
                (((1,), (1,)), ((), ())),
                preferred_element_type=jnp.float32,
            )
            product = product.reshape(rows, height + 2, breadth + 2, 9, narrow)
            part = jnp.zeros((rows, height, breadth, narrow), jnp.float32)
            for b in range(3):
                for c in range(3):
                    part = (
                        part
                        + product[:, 2 - b : 2 - b + height, 2 - c : 2 - c + breadth, b * 3 + c, :]
                    )
            inside = tap_mask(rows, 1 - a)
            total = total + jnp.where(inside, part, jnp.zeros_like(part))
        return (weight_grad, total.reshape(voxels, narrow))

    def layer_sum(weight_grad):
        return lax.psum(weight_grad, "dp")

    plane_one, pre_one = forward(volume, filter_one)
    act_one = leaky(pre_one).astype(jnp.bfloat16).reshape(rows, height, breadth, narrow)
    plane_two, pre_two = forward(act_one, filter_two)
    output = leaky(pre_two).astype(jnp.bfloat16).reshape(rows, height, breadth, narrow)
    delta_two = (cotangent.reshape(voxels, narrow).astype(jnp.float32) * slope_of(pre_two)).astype(
        jnp.bfloat16
    )
    local_two, back_two = backward(
        plane_two, delta_two.reshape(rows, height, breadth, narrow), filter_two
    )
    summed_two = layer_sum(local_two)
    delta_one = (back_two * slope_of(pre_one)).astype(jnp.bfloat16)
    local_one, back_one = backward(
        plane_one, delta_one.reshape(rows, height, breadth, narrow), filter_one
    )
    summed_one = layer_sum(local_one)
    input_grad = back_one.astype(jnp.bfloat16).reshape(rows, height, breadth, narrow)
    return (output, input_grad, summed_one * scale, summed_two * scale)


def is_seam():
    return lax.rem(lax.axis_index("dp") * 2, VOX) == 0


def place():
    at = lax.axis_index("dp")
    return at // 4, lax.rem(at // 2, 2), lax.rem(at, 2)


def place_bits():
    level, side, _ = place()
    return {"x": side, "z": lax.rem(level, 2), "zz": level // 2}


def shaped(values):
    return values.reshape(TILE, VOX, values.shape[1])


PARTS = {
    "all": dict(
        slots=((0, True), (1, True), (2, False), (1, False), (2, True), (3, True)),
        taps=(((0, 0), (1, 1), (2, 2)), ((0, 3), (1, 4), (2, 5))),
    ),
    "local": dict(
        slots=((0, True), (1, True), (0, False), (1, False)),
        taps=(((1, 0), (2, 3)), ((0, 2), (1, 1))),
    ),
    "rim": dict(
        slots=((0, True), (1, True)),
        taps=(((0, 0),), ((2, 1),)),
    ),
}


def filter_rows(kind):
    level, side, core = place()
    along, first = (side, 0) if kind == "quarters" else (lax.rem(level, 2), HALF)
    rows = [] if kind == "quarters" else [(HALF, 0)]
    if kind != "own":
        for unit in (core, 1 - core):
            rows += [(32, first + (2 * at + unit) * 32) for at in (along, 1 - along)]
    return rows


def copy_weights(kind, part, pieces, store, sems):
    me = lax.axis_index("chan")
    copies = []
    for (height, row), piece in zip(filter_rows(kind), pieces):
        if not isinstance(row, int):
            row = pl.multiple_of(row, 32)
        spans = ((0, 27),) if part != "rim" else ((0, 9), (18, 9))
        for side in range(2):
            column = pl.multiple_of((me if side == 0 else 1 - me) * HALF, HALF)
            for first, length in spans:
                taps = pl.ds(first, length)
                copies.append(
                    pltpu.make_async_copy(
                        piece.at[taps, :, pl.ds(column, HALF)],
                        store.at[taps, pl.ds(row, height), pl.ds(side * HALF, HALF)],
                        sems.at[len(copies)],
                    )
                )
    for copy in copies:
        copy.start()
    return copies


def fill_planes(part, planes, store, lane):
    lanes = pl.ds(lane, store.shape[3])
    edge = jnp.zeros(store.shape[2:], store.dtype)
    seam = is_seam()
    for slot, (plane, always) in enumerate(PARTS[part]["slots"]):
        ref, at = planes[plane]
        store[slot, 0] = edge
        store[slot, VOX + 1] = edge
        if always:
            store[slot, 1 : VOX + 1] = ref[at, :, :, lanes]
            continue

        @pl.when(seam)
        def _():
            store[slot] = jnp.zeros(store.shape[1:], store.dtype)

        @pl.when(jnp.logical_not(seam))
        def _():
            store[slot, 1 : VOX + 1] = ref[at, :, :, lanes]


def conv_rows(store, weights, taps, row, flipped, first):
    pieces = []
    for _, slot in taps:
        for b in range(3):
            piece = store[slot, pl.ds(row + b, TILE)]
            pieces.append(piece.reshape(TILE * VOX, store.shape[3]))
    stacked = jnp.concatenate(pieces, axis=1)
    products = []
    for c in range(3):
        if flipped:
            tiles = [weights[(2 - a) * 9 + (2 - b) * 3 + 2 - c] for a, _ in taps for b in range(3)]
            dims = (((1,), (1,)), ((), ()))
            tiles = jnp.concatenate(tiles, axis=1)
        else:
            rows = slice(first, first + store.shape[3])
            tiles = [weights[a * 9 + b * 3 + c, rows] for a, _ in taps for b in range(3)]
            dims = (((1,), (0,)), ((), ()))
            tiles = jnp.concatenate(tiles, axis=0)
        products.append(
            lax.dot_general(stacked, tiles, dims, preferred_element_type=jnp.float32)
        )
    left, middle, right = products
    column = lax.rem(lax.broadcasted_iota(jnp.int32, left.shape, 0), VOX)
    left = jnp.where(column > 0, pltpu.roll(left, 1, 0), 0.0)
    right = jnp.where(column < VOX - 1, pltpu.roll(right, TILE * VOX - 1, 0), 0.0)
    return middle + left + right


def conv_kernel(part, kind, flipped, finish, counts, lane, row, unroll, *refs):
    refs = list(refs)
    groups = []
    for count in counts:
        groups.append(refs[:count])
        refs = refs[count:]
    planes, pieces, begun, extra, outs = groups
    if kind == "ready":
        (weights,), copies = pieces, []
        (store,) = refs
    else:
        store, sems = refs
        weights = outs.pop()
        copies = copy_weights(kind, part, pieces, weights, sems)
    views = []
    for ref in planes:
        views += [(ref, at) for at in range(ref.shape[0])]
    fill_planes(part, views, store, lane)
    for copy in copies:
        copy.wait()
    for plane in range(2):
        taps = PARTS[part]["taps"][plane]

        @pl.loop(0, VOX // TILE, unroll=unroll)
        def _(step):
            rows = pl.ds(pl.multiple_of(step * TILE, TILE), TILE)
            value = shaped(conv_rows(store, weights, taps, step * TILE, flipped, row))
            if begun:
                value = value + begun[0][plane, rows]
            finish(value, plane, rows, extra, outs)


def finish_partial(value, plane, rows, extra, outs):
    outs[0][plane, rows] = value


def finish_first(value, plane, rows, extra, outs):
    outs[plane][0, rows] = leaky(value).astype(jnp.bfloat16)


def finish_second(value, plane, rows, extra, outs):
    output, deltas = outs[0], outs[1:]
    output[plane, rows] = leaky(value[:, :, :HALF]).astype(jnp.bfloat16)
    slope = slope_of(value)
    for lane, cot in ((0, extra[0]), (HALF, extra[1])):
        delta = cot[plane, rows].astype(jnp.float32) * slope[:, :, lane : lane + HALF]
        deltas[plane][0, rows, :, lane : lane + HALF] = delta.astype(jnp.bfloat16)


def finish_back(value, plane, rows, extra, outs):
    act = extra[plane][0, rows].astype(jnp.float32)
    outs[plane][0, rows] = (value * slope_of(act)).astype(jnp.bfloat16)


def finish_last(value, plane, rows, extra, outs):
    outs[0][plane, rows] = value.astype(jnp.bfloat16)


def filter_kernel(colours, *refs):
    low, mid_0, mid_1, high, delta_0, delta_1 = refs[:6]
    outs, (turned, moved) = refs[6:-2], refs[-2:]
    _, _, core = place()
    bits = place_bits()
    pixels = VOX * VOX
    seam = is_seam()
    sources = ((0, low), (1, mid_0), (2, mid_1), (3, high))
    for plane, ref in sources:
        flipped = ref[0].reshape(pixels, HALF).T
        for output_plane in range(2):
            tap = plane - output_plane
            if not 0 <= tap < 3:
                continue
            rows = slice(tap * HALF, (tap + 1) * HALF)
            columns = slice(output_plane * pixels, (output_plane + 1) * pixels)
            if plane in (1, 2) and tap != 1:
                turned[rows, columns] = jnp.where(seam, jnp.zeros_like(flipped), flipped)
            else:
                turned[rows, columns] = flipped
    for plane, ref in ((0, delta_0), (1, delta_1)):
        for c in range(3):
            moved[c, plane, 0] = jnp.zeros(moved.shape[3:], moved.dtype)
            moved[c, plane, VOX + 1] = jnp.zeros(moved.shape[3:], moved.dtype)
        moved[1, plane, 1 : VOX + 1] = ref[0]

        @pl.loop(0, VOX // TILE, unroll=True)
        def _(step):
            row = step * TILE
            values = ref[0, pl.ds(row, TILE)].reshape(TILE * VOX, FULL).astype(jnp.float32)
            column = lax.rem(lax.broadcasted_iota(jnp.int32, values.shape, 0), VOX)
            ahead = jnp.where(column < VOX - 1, pltpu.roll(values, TILE * VOX - 1, 0), 0.0)
            behind = jnp.where(column > 0, pltpu.roll(values, 1, 0), 0.0)
            moved[0, plane, pl.ds(row + 1, TILE)] = shaped(ahead.astype(jnp.bfloat16))
            moved[2, plane, pl.ds(row + 1, TILE)] = shaped(behind.astype(jnp.bfloat16))

    mine = lax.axis_index("chan") == core
    for tap in range(27):
        a, b, c = tap // 9, tap // 3 % 3, tap % 3
        if a:
            continue
        right = moved[c, :, 2 - b : 2 - b + VOX].reshape(2 * pixels, FULL)
        product = jnp.dot(turned[...], right, preferred_element_type=jnp.float32)
        kept = jnp.where(mine, product[:, :HALF], product[:, HALF:])
        sent = jnp.where(mine, product[:, HALF:], product[:, :HALF])
        for a in range(3):
            rows = slice(a * HALF, (a + 1) * HALF)
            for at, (first, taps, axis) in enumerate(colours):
                place_at = a * 9 + b * 3 + c - first
                if not 0 <= place_at < taps:
                    continue
                keep, far, near = outs[3 * at : 3 * at + 3]
                bit = bits[axis]
                keep[:, place_at] = kept[rows].reshape(8, 16, HALF)
                blocks = sent[rows].reshape(2, 4, 16, HALF).astype(far.dtype)
                far[:, place_at] = jnp.where(bit == 0, blocks[1], blocks[0])
                near[:, place_at] = jnp.where(bit == 0, blocks[0], blocks[1])


def halve_core_kernel(axis, keep, far, near, kept, sent):
    bit = place_bits()[axis]
    for target, came, first in ((kept, near, bit * 4), (sent, far, (1 - bit) * 4)):

        @pl.loop(0, 4)
        def _(block):
            total = keep[first + block] + came[block].astype(jnp.float32)
            target[block] = total.astype(target.dtype)


def halve_kernel(axis, keep, came, kept, sent):
    bit = place_bits()[axis]
    half = keep.shape[0] // 2
    for target, first in ((kept, bit * half), (sent, (1 - bit) * half)):
        for block in range(half):
            total = keep[first + block] + came[first + block].astype(jnp.float32)
            target[block] = total.astype(target.dtype)


def finish_kernel(scale, keep, came, total):
    total[...] = ((keep[...] + came[...].astype(jnp.float32)) * scale).astype(total.dtype)


def join_kernel(axis, own, came, target):
    bit = place_bits()[axis]
    half = own.shape[0]
    target[pl.ds(bit * half, half)] = own[...]
    target[pl.ds((1 - bit) * half, half)] = came[...]


def join_core_kernel(order, *refs):
    _, _, core = place()
    grad = refs[-1]
    first_tap = 0
    for own, came in zip(refs[0:-1:2], refs[1:-1:2]):
        base = first_tap
        first_tap += own.shape[1]

        @pl.loop(0, own.shape[1])
        def _(tap):
            for at, block in enumerate(order):
                rows = slice(block * 16, block * 16 + 16)
                first = jnp.where(core == 0, own[at, tap], came[at, tap])
                second = jnp.where(core == 0, came[at, tap], own[at, tap])
                grad[base + tap, rows, :HALF] = first.astype(jnp.float32)
                grad[base + tap, rows, HALF:] = second.astype(jnp.float32)


WEIGHT = {
    "sum_two_core": 0,
    "sum_two_z": 0,
    "sum_two_x": 2 * 10**9,
    "sum_a_core": 0,
    "sum_b_core": 0,
    "first_rim": 3 * 10**9,
    "back_rim": 10**9,
    "sum_a_zz": 2 * 10**9,
    "sum_b_zz": 2 * 10**9,
    "join_a_zz": 2 * 10**9,
    "join_b_zz": 2 * 10**9,
    "join_a_z": 6 * 10**9,
    "join_b_x": 6 * 10**9,
    "join_a_x": 6 * 10**9,
    "join_b_z": 6 * 10**9,
}


def hint(flops):
    return pl.CostEstimate(flops=flops, bytes_accessed=0, transcendentals=0)


def small_call(kernel, outs, operands, name):
    return pl.pallas_call(
        kernel,
        out_shape=[jax.ShapeDtypeStruct(shape, dtype) for shape, dtype in outs],
        in_specs=[pl.BlockSpec(memory_space=pltpu.VMEM)] * len(operands),
        out_specs=[pl.BlockSpec(memory_space=pltpu.VMEM)] * len(outs),
        compiler_params=pltpu.CompilerParams(vmem_limit_bytes=VMEM_LIMIT),
        cost_estimate=hint(WEIGHT.get(name, SMALL)),
        name=name,
    )(*operands)


def halve_core(axis, keep, far, near, name):
    outs = [(far.shape, jnp.float32), (far.shape, jnp.bfloat16)]
    return small_call(functools.partial(halve_core_kernel, axis), outs, [keep, far, near], name)


def halve(axis, keep, came, name):
    shape = (keep.shape[0] // 2,) + keep.shape[1:]
    outs = [(shape, jnp.float32), (shape, jnp.bfloat16)]
    return small_call(functools.partial(halve_kernel, axis), outs, [keep, came], name)


def finish(scale, keep, came, name):
    outs = [(keep.shape, jnp.bfloat16)]
    return small_call(functools.partial(finish_kernel, scale), outs, [keep, came], name)[0]


def join(axis, own, came, name):
    outs = [((2 * own.shape[0],) + own.shape[1:], jnp.bfloat16)]
    return small_call(functools.partial(join_kernel, axis), outs, [own, came], name)[0]


def join_core(order, colours, name):
    outs = [((27, HALF, FULL), jnp.float32)]
    operands = [half for pair in colours for half in pair]
    return small_call(functools.partial(join_core_kernel, order), outs, operands, name)[0]


def conv_call(
    name, part, kind, finish, outs, planes, pieces, begun=(), extra=(), flipped=False,
    lane=0, lanes=None, row=0, unroll=True,
):
    lanes = lanes or planes[0].shape[3]
    height = {"own": HALF, "quarters": HALF, "both": FULL, "ready": pieces[0].shape[1]}[kind]
    ready = kind == "ready"
    if not ready:
        outs = outs + [((27, height, FULL), jnp.bfloat16)]
    operands = [*planes, *pieces, *begun, *extra]
    counts = (len(planes), len(pieces), len(begun), len(extra), len(outs))
    specs = [pl.BlockSpec(memory_space=pltpu.VMEM) for _ in operands]
    if not ready:
        for at in range(len(planes), len(planes) + len(pieces)):
            own = kind != "quarters" and at == len(planes)
            specs[at] = pl.BlockSpec(memory_space=pltpu.HBM if own else pl.ANY)
    scratch = [pltpu.VMEM((len(PARTS[part]["slots"]), VOX + 2, VOX, lanes), jnp.bfloat16)]
    if not ready:
        scratch.append(pltpu.SemaphoreType.DMA((20,)))
    return pl.pallas_call(
        functools.partial(conv_kernel, part, kind, flipped, finish, counts, lane, row, unroll),
        out_shape=[jax.ShapeDtypeStruct(shape, dtype) for shape, dtype in outs],
        in_specs=specs,
        out_specs=[pl.BlockSpec(memory_space=pltpu.VMEM)] * len(outs),
        scratch_shapes=scratch,
        compiler_params=pltpu.CompilerParams(vmem_limit_bytes=VMEM_LIMIT),
        cost_estimate=hint(WEIGHT.get(name, 0)),
        name=name,
    )(*operands)


def filter_call(colours, planes, mid_at, deltas, name):
    narrow = (1, VOX, VOX, HALF)
    specs = [
        pl.BlockSpec(narrow, functools.partial(lambda at, i: (at, 0, 0, 0), at)) for at in mid_at
    ]
    specs += [pl.BlockSpec((1, VOX, VOX, FULL), lambda i: (0, 0, 0, 0))] * 2
    outs = []
    for _, taps, _ in colours:
        for blocks, dtype in ((8, jnp.float32), (4, jnp.bfloat16), (4, jnp.bfloat16)):
            outs.append(jax.ShapeDtypeStruct((blocks, taps, 16, HALF), dtype))
    values = pl.pallas_call(
        functools.partial(filter_kernel, colours),
        grid=(1,),
        out_shape=outs,
        in_specs=specs,
        out_specs=[pl.BlockSpec(out.shape, lambda i: (0, 0, 0, 0)) for out in outs],
        scratch_shapes=[
            pltpu.VMEM((3 * HALF, 2 * VOX * VOX), jnp.bfloat16),
            pltpu.VMEM((3, 2, VOX + 2, VOX, FULL), jnp.bfloat16),
        ],
        compiler_params=pltpu.CompilerParams(vmem_limit_bytes=VMEM_LIMIT),
        cost_estimate=hint(0),
        name=name,
    )(*planes, *deltas)
    return [values[at : at + 3] for at in range(0, len(values), 3)]


def after(value, *earlier):
    return lax.optimization_barrier((value,) + earlier)[0]


def paired(volume, filter_one, filter_two, cotangent):
    count = lax.axis_size("dp")
    ahead = [(i, (i + 1) % count) for i in range(count)]
    behind = [(target, source) for source, target in ahead]
    scale = 1.0 / math.sqrt(count * 2 * VOX * VOX)
    one = filter_one.reshape(27, HALF, FULL)
    two = filter_two.reshape(27, HALF, FULL)
    level, side, core = place()

    def other(values):
        return lax.ppermute(values, "chan", [(0, 1), (1, 0)])

    def to_core(values):
        return lax.ppermute(values, "dp", [(i, i ^ 1) for i in range(count)])

    def to_side(values):
        return lax.ppermute(values, "dp", [(i, i ^ 2) for i in range(count)])

    def to_level(values):
        return lax.ppermute(values, "dp", [(i, i ^ 4) for i in range(count)])

    def to_far_level(values):
        return lax.ppermute(values, "dp", [(i, i ^ 8) for i in range(count)])

    def rims(first, last):
        return lax.ppermute(last, "dp", ahead), lax.ppermute(first, "dp", behind)

    wide = ((1, VOX, VOX, FULL), jnp.bfloat16)
    narrow = ((2, VOX, VOX, HALF), jnp.bfloat16)
    partial = ((2, VOX, VOX, FULL), jnp.float32)
    half_partial = ((2, VOX, VOX, HALF), jnp.float32)

    low_own, high_own = rims(volume[:1], volume[1:])
    one_0 = other(lax.dynamic_slice_in_dim(one, (2 * side + core) * 32, 32, axis=1))
    volume_other = other(after(volume, one_0, low_own, high_own))
    one_1 = to_side(one_0)
    one_2 = to_core(one_0)
    begun, own_ready = conv_call(
        "first_own", "all", "own", finish_partial, [partial], [low_own, volume, high_own], [one],
        unroll=False,
    )
    one_3 = to_core(after(one_1, begun))
    quarters = [one_0, one_1, one_2, one_3]
    volume_other = after(volume_other, begun)
    two_0 = other(
        after(
            lax.dynamic_slice_in_dim(two, (2 * lax.rem(level, 2) + core) * 32, 32, axis=1),
            volume_other,
        )
    )
    low_other, high_other = rims(volume_other[:1], volume_other[1:])
    begun, ready = conv_call(
        "first_other", "local", "quarters", finish_partial, [partial], [volume_other], quarters,
        [begun],
    )
    two_0 = after(two_0, begun)
    two_1 = to_level(two_0)
    two_2 = to_core(two_0)
    cot_other = other(after(cotangent, two_0))
    act_0, act_1 = conv_call(
        "first_rim", "rim", "ready", finish_first, [wide, wide], [low_other, high_other],
        [ready], [begun],
    )
    low_act, high_act = rims(act_0, act_1)
    begun, _ = conv_call(
        "second_own", "local", "own", finish_partial, [partial], [act_0, act_1], [two], lanes=HALF,
        unroll=False,
    )
    two_3 = to_core(after(two_1, begun))
    pieces = [two, two_0, two_1, two_2, two_3]
    begun, ready = conv_call(
        "second_other", "local", "both", finish_partial, [partial], [act_0, act_1], pieces, [begun],
        lane=HALF, lanes=HALF, row=HALF,
    )
    output, delta_0, delta_1 = conv_call(
        "second_rim", "rim", "ready", finish_second, [narrow, wide, wide], [low_act, high_act],
        [ready], [begun], [cotangent, cot_other],
    )
    low_delta, high_delta = rims(delta_0, delta_1)
    ((keep, far, near),) = filter_call(
        ((0, 27, "z"),), [low_act, act_0, act_1, high_act], (0, 0, 0, 0), [delta_0, delta_1],
        "grad_two",
    )
    keep_two, sent = halve_core("z", keep, to_core(far), to_core(near), "sum_two_core")
    came_two = to_level(sent)
    (begun,) = conv_call(
        "back_local", "local", "ready", finish_partial, [partial], [delta_0, after(delta_1, keep_two)],
        [ready], flipped=True,
    )
    prior_0, prior_1 = conv_call(
        "back_rim", "rim", "ready", finish_back, [wide, wide], [low_delta, high_delta],
        [ready], [begun], [act_0, act_1], flipped=True,
    )
    low_prior, high_prior = rims(prior_0, prior_1)
    (keep_a, *sent_a), (keep_b, *sent_b) = filter_call(
        ((0, 14, "x"), (14, 13, "z")), [low_own, volume, volume, high_own], (0, 0, 1, 0),
        [prior_0, prior_1], "grad_one",
    )
    sent_a, sent_b = [to_core(half) for half in sent_a], [to_core(half) for half in sent_b]
    keep_two, sent = halve("x", after(keep_two, keep_a), came_two, "sum_two_z")
    came_two = to_side(sent)
    keep_a, sent = halve_core("x", after(keep_a, keep_two), *sent_a, "sum_a_core")
    came_a = to_side(sent)
    keep_b, sent = halve_core("z", after(keep_b, keep_a), *sent_b, "sum_b_core")
    came_b = to_level(sent)
    (begun,) = conv_call(
        "first_back_local", "local", "ready", finish_partial, [half_partial],
        [after(prior_0, keep_b), prior_1], [own_ready], flipped=True, unroll=False,
    )
    keep_two, sent = halve("zz", after(keep_two, begun, low_prior, high_prior), came_two, "sum_two_x")
    came_two = to_far_level(sent)
    keep_a, sent = halve("z", after(keep_a, keep_two), came_a, "sum_a_x")
    came_a = to_level(sent)
    keep_b, sent = halve("x", after(keep_b, keep_a), came_b, "sum_b_z")
    came_b = to_side(sent)
    own_two = finish(scale, after(keep_two, keep_b), came_two, "sum_two_zz")
    came_two = to_far_level(own_two)
    keep_a, sent = halve("zz", after(keep_a, own_two), came_a, "sum_a_z")
    came_a = to_far_level(sent)
    keep_b, sent = halve("zz", after(keep_b, keep_a), came_b, "sum_b_x")
    came_b = to_far_level(sent)
    own_two = join("zz", after(own_two, keep_b), came_two, "join_two_zz")
    came_two = to_level(own_two)
    own_a = finish(scale, after(keep_a, own_two), came_a, "sum_a_zz")
    came_a = to_far_level(own_a)
    own_b = finish(scale, after(keep_b, own_a), came_b, "sum_b_zz")
    came_b = to_far_level(own_b)
    own_two = join("z", after(own_two, own_b), came_two, "join_two_z")
    came_two = to_side(own_two)
    own_a = join("zz", after(own_a, own_two), came_a, "join_a_zz")
    came_a = to_level(own_a)
    own_b = join("zz", after(own_b, own_a), came_b, "join_b_zz")
    came_b = to_side(own_b)
    own_a = join("z", after(own_a, own_b), came_a, "join_a_z")
    came_a = to_side(own_a)
    own_b = join("x", after(own_b, own_a), came_b, "join_b_x")
    came_b = to_level(own_b)
    (input_grad,) = conv_call(
        "first_back_rim", "rim", "ready", finish_last, [narrow],
        [after(low_prior, own_b), high_prior], [own_ready], [begun], flipped=True,
    )
    own_two = join("x", after(own_two, input_grad), came_two, "join_two_x")
    came_two = to_core(own_two)
    own_a = join("x", after(own_a, own_two), came_a, "join_a_x")
    came_a = to_core(own_a)
    own_b = join("z", after(own_b, own_a), came_b, "join_b_z")
    came_b = to_core(own_b)
    summed_two = join_core(
        (0, 1, 4, 5, 2, 3, 6, 7), [(after(own_two, own_b), came_two)], "grads_two"
    )
    summed_one = join_core(
        tuple(range(8)), [(after(own_a, summed_two), came_a), (own_b, came_b)], "grads_one"
    )
    shape = filter_one.shape
    return output, input_grad, summed_one.reshape(shape), summed_two.reshape(shape)


def local(volume, filter_one, filter_two, cotangent):
    pair = lax.axis_size("chan") == 2 and lax.axis_size("dp") == 16
    if pair and volume.shape == (2, VOX, VOX, HALF):
        return paired(volume, filter_one, filter_two, cotangent)
    return plain(volume, filter_one, filter_two, cotangent)


def solution(mesh):
    in_specs = (
        P("dp", None, None, "chan"),
        P(None, None, None, "chan", None),
        P(None, None, None, "chan", None),
        P("dp", None, None, "chan"),
    )
    out_specs = (
        P("dp", None, None, "chan"),
        P("dp", None, None, "chan"),
        P(None, None, None, "chan", None),
        P(None, None, None, "chan", None),
    )
    return jax.shard_map(local, mesh=mesh, in_specs=in_specs, out_specs=out_specs, check_vma=False)
```

profile of v0, /device:TPU:5, one launch (start us, length us, event | category | flops | bytes accessed | tf_op | source)
XLA Modules:
  0.0 154.4 jit_solution(10711479724508789339)
XLA Ops:
  5.4 3.3 %collective-permute-done.1.refs_0_ = bf16[1,32,32,128]{3,2,1,0:T(8,128)(2,1)S(1)} collective-permute-done((bf16[1,32,32,128]{3,2,1,0:T(8,128)(2,1)S(1)}, bf16[1,32,32,128]{3,2,1,0:T(8,128)(2,1)S(1)}, u32[]{:S(2)}, u32[]{:S(2)}) %collective-permute-start.1) | collective-permute-done | bytes 262176 | tf_op jit(solution)/shard_map/ppermute | solution.py:569
  8.7 5.6 %collective-permute-done.2.refs_2_.refs_3_ = bf16[1,32,32,128]{3,2,1,0:T(8,128)(2,1)S(1)} collective-permute-done((bf16[1,32,32,128]{3,2,1,0:T(8,128)(2,1)S(1)}, bf16[1,32,32,128]{3,2,1,0:T(8,128)(2,1)S(1)}, u32[]{:S(2)}, u32[]{:S(2)}) %collective-permute-start.2) | collective-permute-done | bytes 262176 | tf_op jit(solution)/shard_map/ppermute | solution.py:569
  16.7 5.3 %first_own.1 = (f32[2,32,32,256]{3,2,1,0:T(8,128)S(1)}, bf16[27,128,256]{2,1,0:T(8,128)(2,1)S(1)}) custom-call(bf16[1,32,32,128]{3,2,1,0:T(8,128)(2,1)S(1)} %collective-permute-done.1.refs_0_, bf16[2,32,32,128]{3,2,1,0:T(8,128)(2,1)S(1)} %copy-done.1, bf16[1,32,32,128]{3,2,1,0:T(8,128)(2,1)S(1)} %collective-permute-done.2.refs_2_.refs_3_, ...), custom_call_target="tpu_custom_call" | custom-call | tf_op jit(solution)/shard_map/first_own/pallas_call | solution.py:501
  23.6 3.9 %collective-permute-done.6.refs_2_ = bf16[27,32,256]{2,1,0:T(8,128)(2,1)} collective-permute-done((bf16[27,32,256]{2,1,0:T(8,128)(2,1)}, bf16[27,32,256]{2,1,0:T(8,128)(2,1)}, u32[]{:S(2)}, u32[]{:S(2)}) %collective-permute-start.6) | collective-permute-done | bytes 442400 | tf_op jit(solution)/shard_map/ppermute | solution.py:560
  30.0 4.1 %first_other.1 = (f32[2,32,32,256]{3,2,1,0:T(8,128)S(1)}, bf16[27,128,256]{2,1,0:T(8,128)(2,1)S(1)}) custom-call(bf16[2,32,32,128]{3,2,1,0:T(8,128)(2,1)S(1)} %collective-permute-done.3.refs_0_, bf16[27,32,256]{2,1,0:T(8,128)(2,1)} %collective-permute-done.refs_1_, bf16[27,32,256]{2,1,0:T(8,128)(2,1)} %collective-permute-done.6.refs_2_, ...), custom_call_target="tpu_custom_call" | custom-call | tf_op jit(solution)/shard_map/first_other/pallas_call | solution.py:501
  34.1 5.0 %collective-permute-done.11.refs_3_ = bf16[27,32,256]{2,1,0:T(8,128)(2,1)S(1)} collective-permute-done((bf16[27,32,256]{2,1,0:T(8,128)(2,1)S(1)}, bf16[27,32,256]{2,1,0:T(8,128)(2,1)S(1)}, u32[]{:S(2)}, u32[]{:S(2)}) %collective-permute-start.11) | collective-permute-done | bytes 442400 | tf_op jit(solution)/shard_map/ppermute | solution.py:554
  44.8 4.2 %second_own.1 = (f32[2,32,32,256]{3,2,1,0:T(8,128)S(1)}, bf16[27,128,256]{2,1,0:T(8,128)(2,1)}) custom-call(bf16[1,32,32,256]{3,2,1,0:T(8,128)(2,1)S(1)} %get-tuple-element.84.refs_0_.refs_1_.refs_4_, bf16[1,32,32,256]{3,2,1,0:T(8,128)(2,1)S(1)} %get-tuple-element.83.refs_1_.refs_2_.refs_5_, bf16[27,128,256]{2,1,0:T(8,128)(2,1)S(1)} %bitcast.5), custom_call_target="tpu_custom_call" | custom-call | tf_op jit(solution)/shard_map/second_own/pallas_call | solution.py:501
  53.1 3.8 %second_other.1 = (f32[2,32,32,256]{3,2,1,0:T(8,128)S(1)}, bf16[27,256,256]{2,1,0:T(8,128)(2,1)S(1)}) custom-call(bf16[1,32,32,256]{3,2,1,0:T(8,128)(2,1)S(1)} %get-tuple-element.84.refs_0_.refs_1_.refs_4_, bf16[1,32,32,256]{3,2,1,0:T(8,128)(2,1)S(1)} %get-tuple-element.83.refs_1_.refs_2_.refs_5_, bf16[27,128,256]{2,1,0:T(8,128)(2,1)S(1)} %bitcast.6, ...), custom_call_target="tpu_custom_call" | custom-call | tf_op jit(solution)/shard_map/second_other/pallas_call | solution.py:501
  57.0 3.6 %second_rim.1 = (bf16[2,32,32,128]{3,2,1,0:T(8,128)(2,1)}, bf16[1,32,32,256]{3,2,1,0:T(8,128)(2,1)S(1)}, bf16[1,32,32,256]{3,2,1,0:T(8,128)(2,1)S(1)}) custom-call(bf16[1,32,32,256]{3,2,1,0:T(8,128)(2,1)S(1)} %collective-permute-done.9.refs_0_, bf16[1,32,32,256]{3,2,1,0:T(8,128)(2,1)S(1)} %collective-permute-done.10.refs_1_.refs_3_, ...), custom_call_target="tpu_custom_call" | custom-call | tf_op jit(solution)/shard_map/second_rim/pallas_call | solution.py:501
  62.0 4.0 %grad_two.1 = (f32[8,27,16,128]{3,2,1,0:T(8,128)S(1)}, bf16[4,27,16,128]{3,2,1,0:T(8,128)(2,1)S(1)}, bf16[4,27,16,128]{3,2,1,0:T(8,128)(2,1)S(1)}) custom-call(bf16[1,32,32,256]{3,2,1,0:T(8,128)(2,1)S(1)} %collective-permute-done.9.refs_0_, bf16[1,32,32,256]{3,2,1,0:T(8,128)(2,1)S(1)} %get-tuple-element.84.refs_0_.refs_1_.refs_4_, ...), custom_call_target="tpu_custom_call" | custom-call | tf_op jit(solution)/shard_map/grad_two/pallas_call | solution.py:523
  66.0 4.5 %collective-permute-start.18 = (bf16[4,27,16,128]{3,2,1,0:T(8,128)(2,1)S(1)}, bf16[4,27,16,128]{3,2,1,0:T(8,128)(2,1)S(1)}, u32[]{:S(2)}, u32[]{:S(2)}) collective-permute-start(bf16[4,27,16,128]{3,2,1,0:T(8,128)(2,1)S(1)} %get-tuple-element.96), channel_id=1, source_target_pairs={{0,1},{1,0},{2,3},{3,2},{4,5},{5,4},{6,7},{7,6},{8,9},{9,8},{10,11... | collective-permute-start | bytes 1327112 | tf_op jit(solution)/shard_map/ppermute | solution.py:557
  72.8 5.4 %back_local.1.refs_3_ = f32[2,32,32,256]{3,2,1,0:T(8,128)S(1)} custom-call(bf16[1,32,32,256]{3,2,1,0:T(8,128)(2,1)S(1)} %get-tuple-element.94.refs_4_.refs_0_, bf16[1,32,32,256]{3,2,1,0:T(8,128)(2,1)S(1)} %get-tuple-element.99.refs_5_.refs_1_, bf16[27,256,256]{2,1,0:T(8,128)(2,1)S(1)} %get-tuple-element.89.refs_2_), custom_call_target="tpu_custom_call" | custom-call | tf_op jit(solution)/shard_map/back_local/pallas_call | solution.py:501
  78.3 2.8 %back_rim.1 = (bf16[1,32,32,256]{3,2,1,0:T(8,128)(2,1)S(1)}, bf16[1,32,32,256]{3,2,1,0:T(8,128)(2,1)S(1)}) custom-call(bf16[1,32,32,256]{3,2,1,0:T(8,128)(2,1)S(1)} %collective-permute-done.16.refs_0_, bf16[1,32,32,256]{3,2,1,0:T(8,128)(2,1)S(1)} %collective-permute-done.17.refs_1_, bf16[27,256,256]{2,1,0:T(8,128)(2,1)S(1)} %get-tuple-element.89.refs_2_, ...), custom_call_target="tpu_custom_call" | custom-call | flops 1000000000 | tf_op jit(solution)/shard_map/back_rim/pallas_call | solution.py:501
  81.6 3.9 %grad_one.1 = (f32[8,14,16,128]{3,2,1,0:T(8,128)S(1)}, bf16[4,14,16,128]{3,2,1,0:T(8,128)(2,1)S(1)}, bf16[4,14,16,128]{3,2,1,0:T(8,128)(2,1)S(1)}, f32[8,13,16,1...) custom-call(bf16[1,32,32,128]{3,2,1,0:T(8,128)(2,1)S(1)} %collective-permute-done.1.ref, ...), custom_call_target="tpu_custom_call" | custom-call | tf_op jit(solution)/shard_map/grad_one/pallas_call | solution.py:523
  85.5 5.4 %collective-permute-start.22 = (bf16[4,14,16,128]{3,2,1,0:T(8,128)(2,1)S(1)}, bf16[4,14,16,128]{3,2,1,0:T(8,128)(2,1)S(1)}, u32[]{:S(2)}, u32[]{:S(2)}) collective-permute-start(bf16[4,14,16,128]{3,2,1,0:T(8,128)(2,1)S(1)} %get-tuple-element.108), channel_id=1, source_target_pairs={{0,1},{1,0},{2,3},{3,2},{4,5},{5,4},{6,7},{7,6},{8,9},{9,8},{10,11... | collective-permute-start | bytes 688136 | tf_op jit(solution)/shard_map/ppermute | solution.py:557
  95.9 5.9 %first_back_local.1.refs_3_ = f32[2,32,32,128]{3,2,1,0:T(8,128)S(1)} custom-call(bf16[1,32,32,256]{3,2,1,0:T(8,128)(2,1)S(1)} %get-tuple-element.115.refs_4_.refs_0_, bf16[1,32,32,256]{3,2,1,0:T(8,128)(2,1)S(1)} %get-tuple-element.100.refs_5_.refs_1_, bf16[27,128,256]{2,1,0:T(8,128)(2,1)S(1)} %get-tuple-element.116.refs_2_), custom_call_target="tpu_custom_call" | custom-call | tf_op jit(solution)/shard_map/first_back_local/pallas_call | solution.py:501
  102.0 3.7 %collective-permute-start.30 = (bf16[1,27,16,128]{3,2,1,0:T(8,128)(2,1)S(1)}, bf16[1,27,16,128]{3,2,1,0:T(8,128)(2,1)S(1)}, u32[]{:S(2)}, u32[]{:S(2)}) collective-permute-start(bf16[1,27,16,128]{3,2,1,0:T(8,128)(2,1)S(1)} %get-tuple-element.127), channel_id=1, source_target_pairs={{0,8},{1,9},{2,10},{3,11},{4,12},{5,13},{6,14},{7,15},{8,0},{9,1},... | collective-permute-start | bytes 331784 | tf_op jit(solution)/shard_map/ppermute | solution.py:566
  116.3 3.2 %collective-permute-start.37 = (bf16[1,14,16,128]{3,2,1,0:T(8,128)(2,1)S(1)}, bf16[1,14,16,128]{3,2,1,0:T(8,128)(2,1)S(1)}, u32[]{:S(2)}, u32[]{:S(2)}) collective-permute-start(bf16[1,14,16,128]{3,2,1,0:T(8,128)(2,1)S(1)} %sum_a_zz.1.own), channel_id=1, source_target_pairs={{0,8},{1,9},{2,10},{3,11},{4,12},{5,13},{6,14},{7,15},{8,0},{9,1},... | collective-permute-start | bytes 172040 | tf_op jit(solution)/shard_map/ppermute | solution.py:566
  125.3 5.8 %collective-permute-start.40 = (bf16[2,13,16,128]{3,2,1,0:T(8,128)(2,1)S(1)}, bf16[2,13,16,128]{3,2,1,0:T(8,128)(2,1)S(1)}, u32[]{:S(2)}, u32[]{:S(2)}) collective-permute-start(bf16[2,13,16,128]{3,2,1,0:T(8,128)(2,1)S(1)} %join_b_zz.1.own), channel_id=1, source_target_pairs={{0,2},{1,3},{2,0},{3,1},{4,6},{5,7},{6,4},{7,5},{8,10},{9,11},{10,... | collective-permute-start | bytes 319496 | tf_op jit(solution)/shard_map/ppermute | solution.py:560
  131.2 3.5 %collective-permute-start.42 = (bf16[4,14,16,128]{3,2,1,0:T(8,128)(2,1)S(1)}, bf16[4,14,16,128]{3,2,1,0:T(8,128)(2,1)S(1)}, u32[]{:S(2)}, u32[]{:S(2)}) collective-permute-start(bf16[4,14,16,128]{3,2,1,0:T(8,128)(2,1)S(1)} %join_a_z.1.own), channel_id=1, source_target_pairs={{0,2},{1,3},{2,0},{3,1},{4,6},{5,7},{6,4},{7,5},{8,10},{9,11},{10,... | collective-permute-start | bytes 688136 | tf_op jit(solution)/shard_map/ppermute | solution.py:560
  134.8 3.4 %first_back_rim.1 = bf16[2,32,32,128]{3,2,1,0:T(8,128)(2,1)} custom-call(bf16[1,32,32,256]{3,2,1,0:T(8,128)(2,1)S(1)} %collective-permute-done.20.refs_0_, bf16[1,32,32,256]{3,2,1,0:T(8,128)(2,1)S(1)} %collective-permute-done.26.refs_1_, bf16[27,128,256]{2,1,0:T(8,128)(2,1)S(1)} %get-tuple-element.116.refs_2_, f32[2,32,32,128]{3,2,1,0:T(8,128)S(1)} %first_back_local.1.refs_3_), custom_call_target="tpu_custom_call" | custom-call | tf_op jit(solution)/shard_map/first_back_rim/pallas_call | solution.py:501
  138.2 2.6 %collective-permute-done.41.came = bf16[4,27,16,128]{3,2,1,0:T(8,128)(2,1)S(1)} collective-permute-done((bf16[4,27,16,128]{3,2,1,0:T(8,128)(2,1)S(1)}, bf16[4,27,16,128]{3,2,1,0:T(8,128)(2,1)S(1)}, u32[]{:S(2)}, u32[]{:S(2)}) %collective-permute-start.41) | collective-permute-done | bytes 442400 | tf_op jit(solution)/shard_map/ppermute | solution.py:560
  140.8 6.6 %collective-permute-start.44 = (bf16[8,27,16,128]{3,2,1,0:T(8,128)(2,1)S(1)}, bf16[8,27,16,128]{3,2,1,0:T(8,128)(2,1)S(1)}, u32[]{:S(2)}, u32[]{:S(2)}) collective-permute-start(bf16[8,27,16,128]{3,2,1,0:T(8,128)(2,1)S(1)} %join_two_x.1.refs_0_), channel_id=1, source_target_pairs={{0,1},{1,0},{2,3},{3,2},{4,5},{5,4},{6,7},{7,6},{8,9},{9,8},{10,11... | collective-permute-start | bytes 2654216 | tf_op jit(solution)/shard_map/ppermute | solution.py:557
  147.5 2.4 %collective-permute-start.45 = (bf16[8,14,16,128]{3,2,1,0:T(8,128)(2,1)S(1)}, bf16[8,14,16,128]{3,2,1,0:T(8,128)(2,1)S(1)}, u32[]{:S(2)}, u32[]{:S(2)}) collective-permute-start(bf16[8,14,16,128]{3,2,1,0:T(8,128)(2,1)S(1)} %join_a_x.1.refs_0_), channel_id=1, source_target_pairs={{0,1},{1,0},{2,3},{3,2},{4,5},{5,4},{6,7},{7,6},{8,9},{9,8},{10,11... | collective-permute-start | bytes 1376264 | tf_op jit(solution)/shard_map/ppermute | solution.py:557
  (117 shorter events, 51.6 us)
Async XLA Ops:
  1.9 12.4 %collective-permute-start = (bf16[27,32,256]{2,1,0:T(8,128)(2,1)S(1)}, bf16[27,32,256]{2,1,0:T(8,128)(2,1)}, u32[]{:S(2)}, u32[]{:S(2)}) collective-permute-start(bf16[27,32,256]{2,1,0:T(8,128)(2,1)S(1)} %constant_dynamic-slice_fusion.1), channel_id=1, source_target_pairs={{0,16},{16,0},{1,17},{17,1},{2,18},{18,2},{3,19},{19,3},{4,20},{20... | collective-permute-start | bytes 1327112 | tf_op jit(solution)/shard_map/ppermute | solution.py:554
  5.4 8.9 %collective-permute-start.2 = (bf16[1,32,32,128]{3,2,1,0:T(8,128)(2,1)S(1)}, bf16[1,32,32,128]{3,2,1,0:T(8,128)(2,1)S(1)}, u32[]{:S(2)}, u32[]{:S(2)}) collective-permute-start(bf16[1,32,32,128]{3,2,1,0:T(8,128)(2,1)S(1)} %get-tuple-element.152), channel_id=1, source_target_pairs={{1,0},{2,1},{3,2},{4,3},{5,4},{6,5},{7,6},{8,7},{9,8},{10,9},{11,1... | collective-permute-start | bytes 786440 | tf_op jit(solution)/shard_map/ppermute | solution.py:569
  14.3 13.9 %collective-permute-start.3 = (bf16[2,32,32,128]{3,2,1,0:T(8,128)(2,1)}, bf16[2,32,32,128]{3,2,1,0:T(8,128)(2,1)S(1)}, u32[]{:S(2)}, u32[]{:S(2)}) collective-permute-start(bf16[2,32,32,128]{3,2,1,0:T(8,128)(2,1)} %refs_2_.1), channel_id=1, source_target_pairs={{0,16},{16,0},{1,17},{17,1},{2,18},{18,2},{3,19},{19,3},{4,20},{20... | collective-permute-start | bytes 1572872 | tf_op jit(solution)/shard_map/ppermute | solution.py:554
  15.2 12.3 %collective-permute-start.6 = (bf16[27,32,256]{2,1,0:T(8,128)(2,1)}, bf16[27,32,256]{2,1,0:T(8,128)(2,1)}, u32[]{:S(2)}, u32[]{:S(2)}) collective-permute-start(bf16[27,32,256]{2,1,0:T(8,128)(2,1)} %collective-permute-done.refs_1_), channel_id=1, source_target_pairs={{0,2},{1,3},{2,0},{3,1},{4,6},{5,7},{6,4},{7,5},{8,10},{9,11},{10,... | collective-permute-start | bytes 1327112 | tf_op jit(solution)/shard_map/ppermute | solution.py:560
  28.1 11.0 %collective-permute-start.11 = (bf16[27,32,256]{2,1,0:T(8,128)(2,1)S(1)}, bf16[27,32,256]{2,1,0:T(8,128)(2,1)S(1)}, u32[]{:S(2)}, u32[]{:S(2)}) collective-permute-start(bf16[27,32,256]{2,1,0:T(8,128)(2,1)S(1)} %constant_dynamic-slice_fusion), channel_id=1, source_target_pairs={{0,16},{16,0},{1,17},{17,1},{2,18},{18,2},{3,19},{19,3},{4,20},{20... | collective-permute-start | bytes 1327112 | tf_op jit(solution)/shard_map/ppermute | solution.py:554
  29.2 10.5 %collective-permute-start.4 = (bf16[1,32,32,128]{3,2,1,0:T(8,128)(2,1)S(1)}, bf16[1,32,32,128]{3,2,1,0:T(8,128)(2,1)S(1)}, u32[]{:S(2)}, u32[]{:S(2)}) collective-permute-start(bf16[1,32,32,128]{3,2,1,0:T(8,128)(2,1)S(1)} %get-tuple-element.151), channel_id=1, source_target_pairs={{0,1},{1,2},{2,3},{3,4},{4,5},{5,6},{6,7},{7,8},{8,9},{9,10},{10,1... | collective-permute-start | bytes 786440 | tf_op jit(solution)/shard_map/ppermute | solution.py:569
  29.4 10.3 %collective-permute-start.5 = (bf16[1,32,32,128]{3,2,1,0:T(8,128)(2,1)S(1)}, bf16[1,32,32,128]{3,2,1,0:T(8,128)(2,1)S(1)}, u32[]{:S(2)}, u32[]{:S(2)}) collective-permute-start(bf16[1,32,32,128]{3,2,1,0:T(8,128)(2,1)S(1)} %get-tuple-element.150), channel_id=1, source_target_pairs={{1,0},{2,1},{3,2},{4,3},{5,4},{6,5},{7,6},{8,7},{9,8},{10,9},{11,1... | collective-permute-start | bytes 786440 | tf_op jit(solution)/shard_map/ppermute | solution.py:569
  39.1 11.0 %collective-permute-start.12 = (bf16[27,32,256]{2,1,0:T(8,128)(2,1)S(1)}, bf16[27,32,256]{2,1,0:T(8,128)(2,1)S(1)}, u32[]{:S(2)}, u32[]{:S(2)}) collective-permute-start(bf16[27,32,256]{2,1,0:T(8,128)(2,1)S(1)} %collective-permute-done.11.refs_3_), channel_id=1, source_target_pairs={{0,4},{1,5},{2,6},{3,7},{4,0},{5,1},{6,2},{7,3},{8,12},{9,13},{10,... | collective-permute-start | bytes 1327112 | tf_op jit(solution)/shard_map/ppermute | solution.py:563
  41.7 15.3 %collective-permute-start.10 = (bf16[1,32,32,256]{3,2,1,0:T(8,128)(2,1)S(1)}, bf16[1,32,32,256]{3,2,1,0:T(8,128)(2,1)S(1)}, u32[]{:S(2)}, u32[]{:S(2)}) collective-permute-start(bf16[1,32,32,256]{3,2,1,0:T(8,128)(2,1)S(1)} %get-tuple-element.84.refs_0_.refs_1_.refs_4_), channel_id=1, source_target_pairs={{1,0},{2,1},{3,2},{4,3},{5,4},{6,5},{7,6},{8,7},{9,8},{10,9},{11,1... | collective-permute-start | bytes 1572872 | tf_op jit(solution)/shard_map/ppermute | solution.py:569
  43.5 13.4 %collective-permute-start.9 = (bf16[1,32,32,256]{3,2,1,0:T(8,128)(2,1)S(1)}, bf16[1,32,32,256]{3,2,1,0:T(8,128)(2,1)S(1)}, u32[]{:S(2)}, u32[]{:S(2)}) collective-permute-start(bf16[1,32,32,256]{3,2,1,0:T(8,128)(2,1)S(1)} %get-tuple-element.83.refs_1_.refs_2_.refs_5_), channel_id=1, source_target_pairs={{0,1},{1,2},{2,3},{3,4},{4,5},{5,6},{6,7},{7,8},{8,9},{9,10},{10,1... | collective-permute-start | bytes 1572872 | tf_op jit(solution)/shard_map/ppermute | solution.py:569
  43.6 13.3 %collective-permute-start.15 = (bf16[2,32,32,128]{3,2,1,0:T(8,128)(2,1)S(1)}, bf16[2,32,32,128]{3,2,1,0:T(8,128)(2,1)S(1)}, u32[]{:S(2)}, u32[]{:S(2)}) collective-permute-start(bf16[2,32,32,128]{3,2,1,0:T(8,128)(2,1)S(1)} %copy-done.3), channel_id=1, source_target_pairs={{0,16},{16,0},{1,17},{17,1},{2,18},{18,2},{3,19},{19,3},{4,20},{20... | collective-permute-start | bytes 1572872 | tf_op jit(solution)/shard_map/ppermute | solution.py:554
  60.5 17.7 %collective-permute-start.16 = (bf16[1,32,32,256]{3,2,1,0:T(8,128)(2,1)S(1)}, bf16[1,32,32,256]{3,2,1,0:T(8,128)(2,1)S(1)}, u32[]{:S(2)}, u32[]{:S(2)}) collective-permute-start(bf16[1,32,32,256]{3,2,1,0:T(8,128)(2,1)S(1)} %get-tuple-element.99.refs_5_.refs_1_), channel_id=1, source_target_pairs={{0,1},{1,2},{2,3},{3,4},{4,5},{5,6},{6,7},{7,8},{8,9},{9,10},{10,1... | collective-permute-start | bytes 1572872 | tf_op jit(solution)/shard_map/ppermute | solution.py:569
  61.5 16.8 %collective-permute-start.17 = (bf16[1,32,32,256]{3,2,1,0:T(8,128)(2,1)S(1)}, bf16[1,32,32,256]{3,2,1,0:T(8,128)(2,1)S(1)}, u32[]{:S(2)}, u32[]{:S(2)}) collective-permute-start(bf16[1,32,32,256]{3,2,1,0:T(8,128)(2,1)S(1)} %get-tuple-element.94.refs_4_.refs_0_), channel_id=1, source_target_pairs={{1,0},{2,1},{3,2},{4,3},{5,4},{6,5},{7,6},{8,7},{9,8},{10,9},{11,1... | collective-permute-start | bytes 1572872 | tf_op jit(solution)/shard_map/ppermute | solution.py:569
  72.8 18.2 %collective-permute-start.21 = (bf16[4,27,16,128]{3,2,1,0:T(8,128)(2,1)S(1)}, bf16[4,27,16,128]{3,2,1,0:T(8,128)(2,1)S(1)}, u32[]{:S(2)}, u32[]{:S(2)}) collective-permute-start(bf16[4,27,16,128]{3,2,1,0:T(8,128)(2,1)S(1)} %get-tuple-element.105), channel_id=1, source_target_pairs={{0,4},{1,5},{2,6},{3,7},{4,0},{5,1},{6,2},{7,3},{8,12},{9,13},{10,... | collective-permute-start | bytes 1327112 | tf_op jit(solution)/shard_map/ppermute | solution.py:563
  81.1 20.8 %collective-permute-start.20 = (bf16[1,32,32,256]{3,2,1,0:T(8,128)(2,1)S(1)}, bf16[1,32,32,256]{3,2,1,0:T(8,128)(2,1)S(1)}, u32[]{:S(2)}, u32[]{:S(2)}) collective-permute-start(bf16[1,32,32,256]{3,2,1,0:T(8,128)(2,1)S(1)} %get-tuple-element.100.refs_5_.refs_1_), channel_id=1, source_target_pairs={{0,1},{1,2},{2,3},{3,4},{4,5},{5,6},{6,7},{7,8},{8,9},{9,10},{10,1... | collective-permute-start | bytes 1572872 | tf_op jit(solution)/shard_map/ppermute | solution.py:569
  81.1 20.8 %collective-permute-start.26 = (bf16[1,32,32,256]{3,2,1,0:T(8,128)(2,1)S(1)}, bf16[1,32,32,256]{3,2,1,0:T(8,128)(2,1)S(1)}, u32[]{:S(2)}, u32[]{:S(2)}) collective-permute-start(bf16[1,32,32,256]{3,2,1,0:T(8,128)(2,1)S(1)} %get-tuple-element.115.refs_4_.refs_0_), channel_id=1, source_target_pairs={{1,0},{2,1},{3,2},{4,3},{5,4},{6,5},{7,6},{8,7},{9,8},{10,9},{11,1... | collective-permute-start | bytes 1572872 | tf_op jit(solution)/shard_map/ppermute | solution.py:569
  92.0 9.9 %collective-permute-start.27 = (bf16[2,27,16,128]{3,2,1,0:T(8,128)(2,1)S(1)}, bf16[2,27,16,128]{3,2,1,0:T(8,128)(2,1)S(1)}, u32[]{:S(2)}, u32[]{:S(2)}) collective-permute-start(bf16[2,27,16,128]{3,2,1,0:T(8,128)(2,1)S(1)} %get-tuple-element.118), channel_id=1, source_target_pairs={{0,2},{1,3},{2,0},{3,1},{4,6},{5,7},{6,4},{7,5},{8,10},{9,11},{10,... | collective-permute-start | bytes 663560 | tf_op jit(solution)/shard_map/ppermute | solution.py:560
  92.8 12.8 %collective-permute-start.28 = (bf16[4,14,16,128]{3,2,1,0:T(8,128)(2,1)S(1)}, bf16[4,14,16,128]{3,2,1,0:T(8,128)(2,1)S(1)}, u32[]{:S(2)}, u32[]{:S(2)}) collective-permute-start(bf16[4,14,16,128]{3,2,1,0:T(8,128)(2,1)S(1)} %get-tuple-element.121), channel_id=1, source_target_pairs={{0,2},{1,3},{2,0},{3,1},{4,6},{5,7},{6,4},{7,5},{8,10},{9,11},{10,... | collective-permute-start | bytes 688136 | tf_op jit(solution)/shard_map/ppermute | solution.py:560
  94.4 12.1 %collective-permute-start.29 = (bf16[4,13,16,128]{3,2,1,0:T(8,128)(2,1)S(1)}, bf16[4,13,16,128]{3,2,1,0:T(8,128)(2,1)S(1)}, u32[]{:S(2)}, u32[]{:S(2)}) collective-permute-start(bf16[4,13,16,128]{3,2,1,0:T(8,128)(2,1)S(1)} %get-tuple-element.124), channel_id=1, source_target_pairs={{0,4},{1,5},{2,6},{3,7},{4,0},{5,1},{6,2},{7,3},{8,12},{9,13},{10,... | collective-permute-start | bytes 638984 | tf_op jit(solution)/shard_map/ppermute | solution.py:563
  125.3 9.4 %collective-permute-start.40 = (bf16[2,13,16,128]{3,2,1,0:T(8,128)(2,1)S(1)}, bf16[2,13,16,128]{3,2,1,0:T(8,128)(2,1)S(1)}, u32[]{:S(2)}, u32[]{:S(2)}) collective-permute-start(bf16[2,13,16,128]{3,2,1,0:T(8,128)(2,1)S(1)} %join_b_zz.1.own), channel_id=1, source_target_pairs={{0,2},{1,3},{2,0},{3,1},{4,6},{5,7},{6,4},{7,5},{8,10},{9,11},{10,... | collective-permute-start | bytes 319496 | tf_op jit(solution)/shard_map/ppermute | solution.py:560
  131.1 9.7 %collective-permute-start.41 = (bf16[4,27,16,128]{3,2,1,0:T(8,128)(2,1)S(1)}, bf16[4,27,16,128]{3,2,1,0:T(8,128)(2,1)S(1)}, u32[]{:S(2)}, u32[]{:S(2)}) collective-permute-start(bf16[4,27,16,128]{3,2,1,0:T(8,128)(2,1)S(1)} %join_two_z.1.own), channel_id=1, source_target_pairs={{0,2},{1,3},{2,0},{3,1},{4,6},{5,7},{6,4},{7,5},{8,10},{9,11},{10,... | collective-permute-start | bytes 1327112 | tf_op jit(solution)/shard_map/ppermute | solution.py:560
  131.2 16.2 %collective-permute-start.42 = (bf16[4,14,16,128]{3,2,1,0:T(8,128)(2,1)S(1)}, bf16[4,14,16,128]{3,2,1,0:T(8,128)(2,1)S(1)}, u32[]{:S(2)}, u32[]{:S(2)}) collective-permute-start(bf16[4,14,16,128]{3,2,1,0:T(8,128)(2,1)S(1)} %join_a_z.1.own), channel_id=1, source_target_pairs={{0,2},{1,3},{2,0},{3,1},{4,6},{5,7},{6,4},{7,5},{8,10},{9,11},{10,... | collective-permute-start | bytes 688136 | tf_op jit(solution)/shard_map/ppermute | solution.py:560
  134.7 15.1 %collective-permute-start.43 = (bf16[4,13,16,128]{3,2,1,0:T(8,128)(2,1)S(1)}, bf16[4,13,16,128]{3,2,1,0:T(8,128)(2,1)S(1)}, u32[]{:S(2)}, u32[]{:S(2)}) collective-permute-start(bf16[4,13,16,128]{3,2,1,0:T(8,128)(2,1)S(1)} %join_b_x.1.own), channel_id=1, source_target_pairs={{0,4},{1,5},{2,6},{3,7},{4,0},{5,1},{6,2},{7,3},{8,12},{9,13},{10,... | collective-permute-start | bytes 638984 | tf_op jit(solution)/shard_map/ppermute | solution.py:563
  140.8 9.2 %collective-permute-start.44 = (bf16[8,27,16,128]{3,2,1,0:T(8,128)(2,1)S(1)}, bf16[8,27,16,128]{3,2,1,0:T(8,128)(2,1)S(1)}, u32[]{:S(2)}, u32[]{:S(2)}) collective-permute-start(bf16[8,27,16,128]{3,2,1,0:T(8,128)(2,1)S(1)} %join_two_x.1.refs_0_), channel_id=1, source_target_pairs={{0,1},{1,0},{2,3},{3,2},{4,5},{5,4},{6,7},{7,6},{8,9},{9,8},{10,11... | collective-permute-start | bytes 2654216 | tf_op jit(solution)/shard_map/ppermute | solution.py:557
  (27 other events, 145.0 us)
where the time goes:
time: 155 us; the launch traced here: 154 us
  starting transfers between devices  64.5 us (42%)
  Pallas kernels  53.8 us (35%)
  waiting for transfers between devices  31.2 us (20%)
  local copies, waits for them, and re-layouts  3.82 us (2%)
    pallas_call x10, Pallas kernels, conv_call(): pl.pallas_call(functools.partial(conv_kernel, part, kind, flipped, finish...  40.5 us
    ppermute x13, starting transfers between devices, to_core(): return lax.ppermute(values, 'dp', [(i, i ^ 1) for i in range(count)])  24.7 us
    ppermute x7, starting transfers between devices, to_side(): return lax.ppermute(values, 'dp', [(i, i ^ 2) for i in range(count)])  13.1 us
    ppermute x6, starting transfers between devices, to_far_level(): return lax.ppermute(values, 'dp', [(i, i ^ 8) for i in range(count)])  11.3 us
    ppermute x10, waiting for transfers between devices, rims(): return (lax.ppermute(last, 'dp', ahead), lax.ppermute(first, 'dp', behind))  8.91 us
    pallas_call x2, Pallas kernels, filter_call(): pl.pallas_call(functools.partial(filter_kernel, colours), grid=(1,), out_...  7.88 us
    ppermute x10, starting transfers between devices, rims(): return (lax.ppermute(last, 'dp', ahead), lax.ppermute(first, 'dp', behind))  7.06 us
    ppermute x7, waiting for transfers between devices, to_side(): return lax.ppermute(values, 'dp', [(i, i ^ 2) for i in range(count)])  6.62 us
  transfers between devices with their start and end apart: 47, of which 18 were waited for; matrix products, arithmetic and copies ran while one was open for 1% of the time, Pallas kernels for 31%

commit v1 on v0

--- a/solution.py
+++ b/solution.py
@@ -171,13 +171,16 @@
 
 
 def filter_rows(kind):
-    level, side, core = place()
-    along, first = (side, 0) if kind == "quarters" else (lax.rem(level, 2), HALF)
-    rows = [] if kind == "quarters" else [(HALF, 0)]
-    if kind != "own":
-        for unit in (core, 1 - core):
-            rows += [(32, first + (2 * at + unit) * 32) for at in (along, 1 - along)]
-    return rows
+    _, side, core = place()
+    if kind == "own":
+        return [(HALF, 0)]
+    if kind == "both":
+        return [(HALF, 0)] + [
+            (32, HALF + unit * 64 + at) for unit in (core, 1 - core) for at in (0, 32)
+        ]
+    return [
+        (32, (2 * along + unit) * 32) for unit in (core, 1 - core) for along in (side, 1 - side)
+    ]
 
 
 def copy_weights(kind, part, pieces, store, sems):
@@ -548,7 +551,7 @@
     scale = 1.0 / math.sqrt(count * 2 * VOX * VOX)
     one = filter_one.reshape(27, HALF, FULL)
     two = filter_two.reshape(27, HALF, FULL)
-    level, side, core = place()
+    _, side, core = place()
 
     def other(values):
         return lax.ppermute(values, "chan", [(0, 1), (1, 0)])
@@ -585,32 +588,27 @@
     one_3 = to_core(after(one_1, begun))
     quarters = [one_0, one_1, one_2, one_3]
     volume_other = after(volume_other, begun)
-    two_0 = other(
-        after(
-            lax.dynamic_slice_in_dim(two, (2 * lax.rem(level, 2) + core) * 32, 32, axis=1),
-            volume_other,
-        )
-    )
+    two_came = [
+        other(after(lax.dynamic_slice_in_dim(two, core * 64 + at, 32, axis=1), volume_other))
+        for at in (0, 32)
+    ]
     low_other, high_other = rims(volume_other[:1], volume_other[1:])
     begun, ready = conv_call(
         "first_other", "local", "quarters", finish_partial, [partial], [volume_other], quarters,
         [begun],
     )
-    two_0 = after(two_0, begun)
-    two_1 = to_level(two_0)
-    two_2 = to_core(two_0)
-    cot_other = other(after(cotangent, two_0))
     act_0, act_1 = conv_call(
         "first_rim", "rim", "ready", finish_first, [wide, wide], [low_other, high_other],
         [ready], [begun],
     )
     low_act, high_act = rims(act_0, act_1)
+    cot_other = other(after(cotangent, act_0))
     begun, _ = conv_call(
         "second_own", "local", "own", finish_partial, [partial], [act_0, act_1], [two], lanes=HALF,
         unroll=False,
     )
-    two_3 = to_core(after(two_1, begun))
-    pieces = [two, two_0, two_1, two_2, two_3]
+    two_came = [after(part, begun) for part in two_came]
+    pieces = [two] + two_came + [to_core(part) for part in two_came]
     begun, ready = conv_call(
         "second_other", "local", "both", finish_partial, [partial], [act_0, act_1], pieces, [begun],
         lane=HALF, lanes=HALF, row=HALF,

time: 155 us -> 155 us (level)
  the two profiles are of different devices: /device:TPU:5 before, /device:TPU:0 now
where the time goes in v1:
time: 155 us
  Pallas kernels  55.2 us (36%)
  waiting for transfers between devices  45.1 us (29%)
  starting transfers between devices  44.6 us (29%)
  local copies, waits for them, and re-layouts  8.67 us (6%)
    pallas_call x10, Pallas kernels, conv_call(): pl.pallas_call(functools.partial(conv_kernel, part, kind, flipped, finish...  41.8 us
    ppermute x10, starting transfers between devices, rims(): return (lax.ppermute(last, 'dp', ahead), lax.ppermute(first, 'dp', behind))  18.6 us
    ppermute x6, waiting for transfers between devices, to_far_level(): return lax.ppermute(values, 'dp', [(i, i ^ 8) for i in range(count)])  13.3 us
    ppermute x7, waiting for transfers between devices, to_side(): return lax.ppermute(values, 'dp', [(i, i ^ 2) for i in range(count)])  9.05 us
    pallas_call x2, Pallas kernels, filter_call(): pl.pallas_call(functools.partial(filter_kernel, colours), grid=(1,), out_...  7.88 us
    ppermute x5, starting transfers between devices, other(): return lax.ppermute(values, 'chan', [(0, 1), (1, 0)])  7.86 us
    ppermute x5, waiting for transfers between devices, other(): return lax.ppermute(values, 'chan', [(0, 1), (1, 0)])  7.83 us
    ppermute x6, starting transfers between devices, to_far_level(): return lax.ppermute(values, 'dp', [(i, i ^ 8) for i in range(count)])  7.52 us
  transfers between devices with their start and end apart: 47, of which 24 were waited for; matrix products, arithmetic and copies ran while one was open for 1% of the time, Pallas kernels for 32%

profile of v1, /device:TPU:0, one launch (start us, length us, event | category | flops | bytes accessed | tf_op | source)
XLA Modules:
  0.0 154.7 jit_solution(9561906905495528012)
XLA Ops:
  1.8 3.0 %collective-permute-start = (bf16[27,32,256]{2,1,0:T(8,128)(2,1)S(1)}, bf16[27,32,256]{2,1,0:T(8,128)(2,1)}, u32[]{:S(2)}, u32[]{:S(2)}) collective-permute-start(bf16[27,32,256]{2,1,0:T(8,128)(2,1)S(1)} %constant_dynamic-slice_fusion.2), channel_id=1, source_target_pairs={{0,16},{16,0},{1,17},{17,1},{2,18},{18,2},{3,19},{19,3},{4,20},{20... | collective-permute-start | bytes 1327112 | tf_op jit(solution)/shard_map/ppermute | solution.py:557
  6.0 4.4 %collective-permute-start.2 = (bf16[1,32,32,128]{3,2,1,0:T(8,128)(2,1)S(1)}, bf16[1,32,32,128]{3,2,1,0:T(8,128)(2,1)S(1)}, u32[]{:S(2)}, u32[]{:S(2)}) collective-permute-start(bf16[1,32,32,128]{3,2,1,0:T(8,128)(2,1)S(1)} %get-tuple-element.156), channel_id=1, source_target_pairs={{1,0},{2,1},{3,2},{4,3},{5,4},{6,5},{7,6},{8,7},{9,8},{10,9},{11,1... | collective-permute-start | bytes 786440 | tf_op jit(solution)/shard_map/ppermute | solution.py:572
  10.4 4.2 %collective-permute-done.1.refs_0_ = bf16[1,32,32,128]{3,2,1,0:T(8,128)(2,1)S(1)} collective-permute-done((bf16[1,32,32,128]{3,2,1,0:T(8,128)(2,1)S(1)}, bf16[1,32,32,128]{3,2,1,0:T(8,128)(2,1)S(1)}, u32[]{:S(2)}, u32[]{:S(2)}) %collective-permute-start.1) | collective-permute-done | bytes 262176 | tf_op jit(solution)/shard_map/ppermute | solution.py:572
  19.8 5.4 %first_own.1 = (f32[2,32,32,256]{3,2,1,0:T(8,128)S(1)}, bf16[27,128,256]{2,1,0:T(8,128)(2,1)S(1)}) custom-call(bf16[1,32,32,128]{3,2,1,0:T(8,128)(2,1)S(1)} %collective-permute-done.1.refs_0_, bf16[2,32,32,128]{3,2,1,0:T(8,128)(2,1)S(1)} %copy-done.1, bf16[1,32,32,128]{3,2,1,0:T(8,128)(2,1)S(1)} %collective-permute-done.2.refs_2_.refs_3_, ...), custom_call_target="tpu_custom_call" | custom-call | tf_op jit(solution)/shard_map/first_own/pallas_call | solution.py:504
  30.9 4.3 %collective-permute-start.5 = (bf16[1,32,32,128]{3,2,1,0:T(8,128)(2,1)}, bf16[1,32,32,128]{3,2,1,0:T(8,128)(2,1)}, u32[]{:S(2)}, u32[]{:S(2)}) collective-permute-start(bf16[1,32,32,128]{3,2,1,0:T(8,128)(2,1)} %get-tuple-element.154), channel_id=1, source_target_pairs={{1,0},{2,1},{3,2},{4,3},{5,4},{6,5},{7,6},{8,7},{9,8},{10,9},{11,1... | collective-permute-start | bytes 786440 | tf_op jit(solution)/shard_map/ppermute | solution.py:572
  39.0 4.3 %first_other.1 = (f32[2,32,32,256]{3,2,1,0:T(8,128)S(1)}, bf16[27,128,256]{2,1,0:T(8,128)(2,1)S(1)}) custom-call(bf16[2,32,32,128]{3,2,1,0:T(8,128)(2,1)S(1)} %collective-permute-done.3.refs_0_, bf16[27,32,256]{2,1,0:T(8,128)(2,1)} %collective-permute-done.refs_1_, bf16[27,32,256]{2,1,0:T(8,128)(2,1)} %collective-permute-done.6.refs_2_, ...), custom_call_target="tpu_custom_call" | custom-call | tf_op jit(solution)/shard_map/first_other/pallas_call | solution.py:504
  43.4 3.0 %first_rim.1 = (bf16[1,32,32,256]{3,2,1,0:T(8,128)(2,1)S(1)}, bf16[1,32,32,256]{3,2,1,0:T(8,128)(2,1)S(1)}) custom-call(bf16[1,32,32,128]{3,2,1,0:T(8,128)(2,1)} %collective-permute-done.4.refs_0_, bf16[1,32,32,128]{3,2,1,0:T(8,128)(2,1)} %collective-permute-done.5.refs_1_, bf16[27,128,256]{2,1,0:T(8,128)(2,1)S(1)} %get-tuple-element.82.refs_2_, ...), custom_call_target="tpu_custom_call" | custom-call | flops 3000000000 | tf_op jit(solution)/shard_map/first_rim/pallas_call | solution.py:504
  48.1 4.2 %second_own.1 = (f32[2,32,32,256]{3,2,1,0:T(8,128)S(1)}, bf16[27,128,256]{2,1,0:T(8,128)(2,1)}) custom-call(bf16[1,32,32,256]{3,2,1,0:T(8,128)(2,1)S(1)} %get-tuple-element.85.refs_0_.refs_1_.refs_4_, bf16[1,32,32,256]{3,2,1,0:T(8,128)(2,1)S(1)} %get-tuple-element.84.refs_1_.refs_2_.refs_5_, bf16[27,128,256]{2,1,0:T(8,128)(2,1)S(1)} %bitcast.5), custom_call_target="tpu_custom_call" | custom-call | tf_op jit(solution)/shard_map/second_own/pallas_call | solution.py:504
  52.4 4.2 %collective-permute-done.11.refs_3_ = bf16[27,32,256]{2,1,0:T(8,128)(2,1)S(1)} collective-permute-done((bf16[27,32,256]{2,1,0:T(8,128)(2,1)S(1)}, bf16[27,32,256]{2,1,0:T(8,128)(2,1)S(1)}, u32[]{:S(2)}, u32[]{:S(2)}) %collective-permute-start.11) | collective-permute-done | bytes 442400 | tf_op jit(solution)/shard_map/ppermute | solution.py:557
  58.5 3.8 %second_other.1 = (f32[2,32,32,256]{3,2,1,0:T(8,128)S(1)}, bf16[27,256,256]{2,1,0:T(8,128)(2,1)S(1)}) custom-call(bf16[1,32,32,256]{3,2,1,0:T(8,128)(2,1)S(1)} %get-tuple-element.85.refs_0_.refs_1_.refs_4_, bf16[1,32,32,256]{3,2,1,0:T(8,128)(2,1)S(1)} %get-tuple-element.84.refs_1_.refs_2_.refs_5_, bf16[27,128,256]{2,1,0:T(8,128)(2,1)S(1)} %bitcast.6, ...), custom_call_target="tpu_custom_call" | custom-call | tf_op jit(solution)/shard_map/second_other/pallas_call | solution.py:504
  64.4 3.6 %second_rim.1 = (bf16[2,32,32,128]{3,2,1,0:T(8,128)(2,1)}, bf16[1,32,32,256]{3,2,1,0:T(8,128)(2,1)S(1)}, bf16[1,32,32,256]{3,2,1,0:T(8,128)(2,1)S(1)}) custom-call(bf16[1,32,32,256]{3,2,1,0:T(8,128)(2,1)S(1)} %collective-permute-done.9.refs_0_, bf16[1,32,32,256]{3,2,1,0:T(8,128)(2,1)S(1)} %collective-permute-done.10.refs_1_.refs_3_, ...), custom_call_target="tpu_custom_call" | custom-call | tf_op jit(solution)/shard_map/second_rim/pallas_call | solution.py:504
  67.9 4.4 %collective-permute-start.17 = (bf16[1,32,32,256]{3,2,1,0:T(8,128)(2,1)S(1)}, bf16[1,32,32,256]{3,2,1,0:T(8,128)(2,1)S(1)}, u32[]{:S(2)}, u32[]{:S(2)}) collective-permute-start(bf16[1,32,32,256]{3,2,1,0:T(8,128)(2,1)S(1)} %get-tuple-element.96.refs_4_.refs_0_), channel_id=1, source_target_pairs={{1,0},{2,1},{3,2},{4,3},{5,4},{6,5},{7,6},{8,7},{9,8},{10,9},{11,1... | collective-permute-start | bytes 1572872 | tf_op jit(solution)/shard_map/ppermute | solution.py:572
  72.4 4.0 %grad_two.1 = (f32[8,27,16,128]{3,2,1,0:T(8,128)S(1)}, bf16[4,27,16,128]{3,2,1,0:T(8,128)(2,1)S(1)}, bf16[4,27,16,128]{3,2,1,0:T(8,128)(2,1)S(1)}) custom-call(bf16[1,32,32,256]{3,2,1,0:T(8,128)(2,1)S(1)} %collective-permute-done.9.refs_0_, bf16[1,32,32,256]{3,2,1,0:T(8,128)(2,1)S(1)} %get-tuple-element.85.refs_0_.refs_1_.refs_4_, ...), custom_call_target="tpu_custom_call" | custom-call | tf_op jit(solution)/shard_map/grad_two/pallas_call | solution.py:526
  79.2 5.4 %back_local.1.refs_3_ = f32[2,32,32,256]{3,2,1,0:T(8,128)S(1)} custom-call(bf16[1,32,32,256]{3,2,1,0:T(8,128)(2,1)S(1)} %get-tuple-element.96.refs_4_.refs_0_, bf16[1,32,32,256]{3,2,1,0:T(8,128)(2,1)S(1)} %get-tuple-element.101.refs_5_.refs_1_, bf16[27,256,256]{2,1,0:T(8,128)(2,1)S(1)} %get-tuple-element.91.refs_2_), custom_call_target="tpu_custom_call" | custom-call | tf_op jit(solution)/shard_map/back_local/pallas_call | solution.py:504
  84.6 2.8 %back_rim.1 = (bf16[1,32,32,256]{3,2,1,0:T(8,128)(2,1)S(1)}, bf16[1,32,32,256]{3,2,1,0:T(8,128)(2,1)S(1)}) custom-call(bf16[1,32,32,256]{3,2,1,0:T(8,128)(2,1)S(1)} %collective-permute-done.16.refs_0_, bf16[1,32,32,256]{3,2,1,0:T(8,128)(2,1)S(1)} %collective-permute-done.17.refs_1_, bf16[27,256,256]{2,1,0:T(8,128)(2,1)S(1)} %get-tuple-element.91.refs_2_, ...), custom_call_target="tpu_custom_call" | custom-call | flops 1000000000 | tf_op jit(solution)/shard_map/back_rim/pallas_call | solution.py:504
  87.6 4.3 %collective-permute-start.26 = (bf16[1,32,32,256]{3,2,1,0:T(8,128)(2,1)S(1)}, bf16[1,32,32,256]{3,2,1,0:T(8,128)(2,1)S(1)}, u32[]{:S(2)}, u32[]{:S(2)}) collective-permute-start(bf16[1,32,32,256]{3,2,1,0:T(8,128)(2,1)S(1)} %get-tuple-element.117.refs_4_.refs_0_), channel_id=1, source_target_pairs={{1,0},{2,1},{3,2},{4,3},{5,4},{6,5},{7,6},{8,7},{9,8},{10,9},{11,1... | collective-permute-start | bytes 1572872 | tf_op jit(solution)/shard_map/ppermute | solution.py:572
  91.9 3.9 %grad_one.1 = (f32[8,14,16,128]{3,2,1,0:T(8,128)S(1)}, bf16[4,14,16,128]{3,2,1,0:T(8,128)(2,1)S(1)}, bf16[4,14,16,128]{3,2,1,0:T(8,128)(2,1)S(1)}, f32[8,13,16,1...) custom-call(bf16[1,32,32,128]{3,2,1,0:T(8,128)(2,1)S(1)} %collective-permute-done.1.ref, ...), custom_call_target="tpu_custom_call" | custom-call | tf_op jit(solution)/shard_map/grad_one/pallas_call | solution.py:526
  100.0 5.9 %first_back_local.1.refs_3_ = f32[2,32,32,128]{3,2,1,0:T(8,128)S(1)} custom-call(bf16[1,32,32,256]{3,2,1,0:T(8,128)(2,1)S(1)} %get-tuple-element.117.refs_4_.refs_0_, bf16[1,32,32,256]{3,2,1,0:T(8,128)(2,1)S(1)} %get-tuple-element.102.refs_5_.refs_1_, bf16[27,128,256]{2,1,0:T(8,128)(2,1)S(1)} %copy-done.3), custom_call_target="tpu_custom_call" | custom-call | tf_op jit(solution)/shard_map/first_back_local/pallas_call | solution.py:504
  105.9 4.1 %collective-permute-done.27.came = bf16[2,27,16,128]{3,2,1,0:T(8,128)(2,1)S(1)} collective-permute-done((bf16[2,27,16,128]{3,2,1,0:T(8,128)(2,1)S(1)}, bf16[2,27,16,128]{3,2,1,0:T(8,128)(2,1)S(1)}, u32[]{:S(2)}, u32[]{:S(2)}) %collective-permute-start.27) | collective-permute-done | bytes 221216 | tf_op jit(solution)/shard_map/ppermute | solution.py:563
  113.7 5.1 %collective-permute-done.30.came = bf16[1,27,16,128]{3,2,1,0:T(8,128)(2,1)S(1)} collective-permute-done((bf16[1,27,16,128]{3,2,1,0:T(8,128)(2,1)S(1)}, bf16[1,27,16,128]{3,2,1,0:T(8,128)(2,1)S(1)}, u32[]{:S(2)}, u32[]{:S(2)}) %collective-permute-start.30) | collective-permute-done | bytes 110624 | tf_op jit(solution)/shard_map/ppermute | solution.py:569
  119.0 2.9 %collective-permute-start.34 = (bf16[1,14,16,128]{3,2,1,0:T(8,128)(2,1)S(1)}, bf16[1,14,16,128]{3,2,1,0:T(8,128)(2,1)S(1)}, u32[]{:S(2)}, u32[]{:S(2)}) collective-permute-start(bf16[1,14,16,128]{3,2,1,0:T(8,128)(2,1)S(1)} %get-tuple-element.138), channel_id=1, source_target_pairs={{0,8},{1,9},{2,10},{3,11},{4,12},{5,13},{6,14},{7,15},{8,0},{9,1},... | collective-permute-start | bytes 172040 | tf_op jit(solution)/shard_map/ppermute | solution.py:569
  122.0 5.6 %collective-permute-done.33.came = bf16[1,27,16,128]{3,2,1,0:T(8,128)(2,1)S(1)} collective-permute-done((bf16[1,27,16,128]{3,2,1,0:T(8,128)(2,1)S(1)}, bf16[1,27,16,128]{3,2,1,0:T(8,128)(2,1)S(1)}, u32[]{:S(2)}, u32[]{:S(2)}) %collective-permute-start.33) | collective-permute-done | bytes 110624 | tf_op jit(solution)/shard_map/ppermute | solution.py:569
  137.7 3.4 %collective-permute-done.39.came = bf16[2,14,16,128]{3,2,1,0:T(8,128)(2,1)S(1)} collective-permute-done((bf16[2,14,16,128]{3,2,1,0:T(8,128)(2,1)S(1)}, bf16[2,14,16,128]{3,2,1,0:T(8,128)(2,1)S(1)}, u32[]{:S(2)}, u32[]{:S(2)}) %collective-permute-start.39) | collective-permute-done | bytes 114720 | tf_op jit(solution)/shard_map/ppermute | solution.py:566
  143.3 3.4 %first_back_rim.1 = bf16[2,32,32,128]{3,2,1,0:T(8,128)(2,1)} custom-call(bf16[1,32,32,256]{3,2,1,0:T(8,128)(2,1)S(1)} %collective-permute-done.20.refs_0_, bf16[1,32,32,256]{3,2,1,0:T(8,128)(2,1)S(1)} %collective-permute-done.26.refs_1_, bf16[27,128,256]{2,1,0:T(8,128)(2,1)S(1)} %copy-done.3, f32[2,32,32,128]{3,2,1,0:T(8,128)S(1)} %first_back_local.1.refs_3_), custom_call_target="tpu_custom_call" | custom-call | tf_op jit(solution)/shard_map/first_back_rim/pallas_call | solution.py:504
  (125 shorter events, 53.8 us)
Async XLA Ops:
  1.8 13.3 %collective-permute-start = (bf16[27,32,256]{2,1,0:T(8,128)(2,1)S(1)}, bf16[27,32,256]{2,1,0:T(8,128)(2,1)}, u32[]{:S(2)}, u32[]{:S(2)}) collective-permute-start(bf16[27,32,256]{2,1,0:T(8,128)(2,1)S(1)} %constant_dynamic-slice_fusion.2), channel_id=1, source_target_pairs={{0,16},{16,0},{1,17},{17,1},{2,18},{18,2},{3,19},{19,3},{4,20},{20... | collective-permute-start | bytes 1327112 | tf_op jit(solution)/shard_map/ppermute | solution.py:557
  5.9 8.7 %collective-permute-start.1 = (bf16[1,32,32,128]{3,2,1,0:T(8,128)(2,1)S(1)}, bf16[1,32,32,128]{3,2,1,0:T(8,128)(2,1)S(1)}, u32[]{:S(2)}, u32[]{:S(2)}) collective-permute-start(bf16[1,32,32,128]{3,2,1,0:T(8,128)(2,1)S(1)} %get-tuple-element.157), channel_id=1, source_target_pairs={{0,1},{1,2},{2,3},{3,4},{4,5},{5,6},{6,7},{7,8},{8,9},{9,10},{10,1... | collective-permute-start | bytes 786440 | tf_op jit(solution)/shard_map/ppermute | solution.py:572
  15.1 14.9 %collective-permute-start.3 = (bf16[2,32,32,128]{3,2,1,0:T(8,128)(2,1)}, bf16[2,32,32,128]{3,2,1,0:T(8,128)(2,1)S(1)}, u32[]{:S(2)}, u32[]{:S(2)}) collective-permute-start(bf16[2,32,32,128]{3,2,1,0:T(8,128)(2,1)} %refs_2_.1), channel_id=1, source_target_pairs={{0,16},{16,0},{1,17},{17,1},{2,18},{18,2},{3,19},{19,3},{4,20},{20... | collective-permute-start | bytes 1572872 | tf_op jit(solution)/shard_map/ppermute | solution.py:557
  16.8 12.2 %collective-permute-start.6 = (bf16[27,32,256]{2,1,0:T(8,128)(2,1)}, bf16[27,32,256]{2,1,0:T(8,128)(2,1)}, u32[]{:S(2)}, u32[]{:S(2)}) collective-permute-start(bf16[27,32,256]{2,1,0:T(8,128)(2,1)} %collective-permute-done.refs_1_), channel_id=1, source_target_pairs={{0,2},{1,3},{2,0},{3,1},{4,6},{5,7},{6,4},{7,5},{8,10},{9,11},{10,... | collective-permute-start | bytes 1327112 | tf_op jit(solution)/shard_map/ppermute | solution.py:563
  18.3 18.1 %collective-permute-start.7 = (bf16[27,32,256]{2,1,0:T(8,128)(2,1)}, bf16[27,32,256]{2,1,0:T(8,128)(2,1)}, u32[]{:S(2)}, u32[]{:S(2)}) collective-permute-start(bf16[27,32,256]{2,1,0:T(8,128)(2,1)} %collective-permute-done.refs_1_), channel_id=1, source_target_pairs={{0,1},{1,0},{2,3},{3,2},{4,5},{5,4},{6,7},{7,6},{8,9},{9,8},{10,11... | collective-permute-start | bytes 1327112 | tf_op jit(solution)/shard_map/ppermute | solution.py:560
  30.8 12.5 %collective-permute-start.4 = (bf16[1,32,32,128]{3,2,1,0:T(8,128)(2,1)}, bf16[1,32,32,128]{3,2,1,0:T(8,128)(2,1)}, u32[]{:S(2)}, u32[]{:S(2)}) collective-permute-start(bf16[1,32,32,128]{3,2,1,0:T(8,128)(2,1)} %get-tuple-element.155), channel_id=1, source_target_pairs={{0,1},{1,2},{2,3},{3,4},{4,5},{5,6},{6,7},{7,8},{8,9},{9,10},{10,1... | collective-permute-start | bytes 786440 | tf_op jit(solution)/shard_map/ppermute | solution.py:572
  30.9 12.4 %collective-permute-start.5 = (bf16[1,32,32,128]{3,2,1,0:T(8,128)(2,1)}, bf16[1,32,32,128]{3,2,1,0:T(8,128)(2,1)}, u32[]{:S(2)}, u32[]{:S(2)}) collective-permute-start(bf16[1,32,32,128]{3,2,1,0:T(8,128)(2,1)} %get-tuple-element.154), channel_id=1, source_target_pairs={{1,0},{2,1},{3,2},{4,3},{5,4},{6,5},{7,6},{8,7},{9,8},{10,9},{11,1... | collective-permute-start | bytes 786440 | tf_op jit(solution)/shard_map/ppermute | solution.py:572
  35.3 17.0 %collective-permute-start.12 = (bf16[27,32,256]{2,1,0:T(8,128)(2,1)S(1)}, bf16[27,32,256]{2,1,0:T(8,128)(2,1)S(1)}, u32[]{:S(2)}, u32[]{:S(2)}) collective-permute-start(bf16[27,32,256]{2,1,0:T(8,128)(2,1)S(1)} %get-tuple-element.89), channel_id=1, source_target_pairs={{0,16},{16,0},{1,17},{17,1},{2,18},{18,2},{3,19},{19,3},{4,20},{20... | collective-permute-start | bytes 1327112 | tf_op jit(solution)/shard_map/ppermute | solution.py:557
  36.4 20.3 %collective-permute-start.11 = (bf16[27,32,256]{2,1,0:T(8,128)(2,1)S(1)}, bf16[27,32,256]{2,1,0:T(8,128)(2,1)S(1)}, u32[]{:S(2)}, u32[]{:S(2)}) collective-permute-start(bf16[27,32,256]{2,1,0:T(8,128)(2,1)S(1)} %get-tuple-element.86), channel_id=1, source_target_pairs={{0,16},{16,0},{1,17},{17,1},{2,18},{18,2},{3,19},{19,3},{4,20},{20... | collective-permute-start | bytes 1327112 | tf_op jit(solution)/shard_map/ppermute | solution.py:557
  46.4 18.0 %collective-permute-start.10 = (bf16[1,32,32,256]{3,2,1,0:T(8,128)(2,1)S(1)}, bf16[1,32,32,256]{3,2,1,0:T(8,128)(2,1)S(1)}, u32[]{:S(2)}, u32[]{:S(2)}) collective-permute-start(bf16[1,32,32,256]{3,2,1,0:T(8,128)(2,1)S(1)} %get-tuple-element.85.refs_0_.refs_1_.refs_4_), channel_id=1, source_target_pairs={{1,0},{2,1},{3,2},{4,3},{5,4},{6,5},{7,6},{8,7},{9,8},{10,9},{11,1... | collective-permute-start | bytes 1572872 | tf_op jit(solution)/shard_map/ppermute | solution.py:572
  47.1 17.3 %collective-permute-start.15 = (bf16[2,32,32,128]{3,2,1,0:T(8,128)(2,1)S(1)}, bf16[2,32,32,128]{3,2,1,0:T(8,128)(2,1)S(1)}, u32[]{:S(2)}, u32[]{:S(2)}) collective-permute-start(bf16[2,32,32,128]{3,2,1,0:T(8,128)(2,1)S(1)} %copy-done.7), channel_id=1, source_target_pairs={{0,16},{16,0},{1,17},{17,1},{2,18},{18,2},{3,19},{19,3},{4,20},{20... | collective-permute-start | bytes 1572872 | tf_op jit(solution)/shard_map/ppermute | solution.py:557
  48.1 16.3 %collective-permute-start.9 = (bf16[1,32,32,256]{3,2,1,0:T(8,128)(2,1)S(1)}, bf16[1,32,32,256]{3,2,1,0:T(8,128)(2,1)S(1)}, u32[]{:S(2)}, u32[]{:S(2)}) collective-permute-start(bf16[1,32,32,256]{3,2,1,0:T(8,128)(2,1)S(1)} %get-tuple-element.84.refs_1_.refs_2_.refs_5_), channel_id=1, source_target_pairs={{0,1},{1,2},{2,3},{3,4},{4,5},{5,6},{6,7},{7,8},{8,9},{9,10},{10,1... | collective-permute-start | bytes 1572872 | tf_op jit(solution)/shard_map/ppermute | solution.py:572
  67.9 16.7 %collective-permute-start.16 = (bf16[1,32,32,256]{3,2,1,0:T(8,128)(2,1)S(1)}, bf16[1,32,32,256]{3,2,1,0:T(8,128)(2,1)S(1)}, u32[]{:S(2)}, u32[]{:S(2)}) collective-permute-start(bf16[1,32,32,256]{3,2,1,0:T(8,128)(2,1)S(1)} %get-tuple-element.101.refs_5_.refs_1_), channel_id=1, source_target_pairs={{0,1},{1,2},{2,3},{3,4},{4,5},{5,6},{6,7},{7,8},{8,9},{9,10},{10,1... | collective-permute-start | bytes 1572872 | tf_op jit(solution)/shard_map/ppermute | solution.py:572
  67.9 16.7 %collective-permute-start.17 = (bf16[1,32,32,256]{3,2,1,0:T(8,128)(2,1)S(1)}, bf16[1,32,32,256]{3,2,1,0:T(8,128)(2,1)S(1)}, u32[]{:S(2)}, u32[]{:S(2)}) collective-permute-start(bf16[1,32,32,256]{3,2,1,0:T(8,128)(2,1)S(1)} %get-tuple-element.96.refs_4_.refs_0_), channel_id=1, source_target_pairs={{1,0},{2,1},{3,2},{4,3},{5,4},{6,5},{7,6},{8,7},{9,8},{10,9},{11,1... | collective-permute-start | bytes 1572872 | tf_op jit(solution)/shard_map/ppermute | solution.py:572
  79.1 17.3 %collective-permute-start.21 = (bf16[4,27,16,128]{3,2,1,0:T(8,128)(2,1)S(1)}, bf16[4,27,16,128]{3,2,1,0:T(8,128)(2,1)S(1)}, u32[]{:S(2)}, u32[]{:S(2)}) collective-permute-start(bf16[4,27,16,128]{3,2,1,0:T(8,128)(2,1)S(1)} %get-tuple-element.107), channel_id=1, source_target_pairs={{0,4},{1,5},{2,6},{3,7},{4,0},{5,1},{6,2},{7,3},{8,12},{9,13},{10,... | collective-permute-start | bytes 1327112 | tf_op jit(solution)/shard_map/ppermute | solution.py:566
  87.4 18.5 %collective-permute-start.20 = (bf16[1,32,32,256]{3,2,1,0:T(8,128)(2,1)S(1)}, bf16[1,32,32,256]{3,2,1,0:T(8,128)(2,1)S(1)}, u32[]{:S(2)}, u32[]{:S(2)}) collective-permute-start(bf16[1,32,32,256]{3,2,1,0:T(8,128)(2,1)S(1)} %get-tuple-element.102.refs_5_.refs_1_), channel_id=1, source_target_pairs={{0,1},{1,2},{2,3},{3,4},{4,5},{5,6},{6,7},{7,8},{8,9},{9,10},{10,1... | collective-permute-start | bytes 1572872 | tf_op jit(solution)/shard_map/ppermute | solution.py:572
  87.6 18.3 %collective-permute-start.26 = (bf16[1,32,32,256]{3,2,1,0:T(8,128)(2,1)S(1)}, bf16[1,32,32,256]{3,2,1,0:T(8,128)(2,1)S(1)}, u32[]{:S(2)}, u32[]{:S(2)}) collective-permute-start(bf16[1,32,32,256]{3,2,1,0:T(8,128)(2,1)S(1)} %get-tuple-element.117.refs_4_.refs_0_), channel_id=1, source_target_pairs={{1,0},{2,1},{3,2},{4,3},{5,4},{6,5},{7,6},{8,7},{9,8},{10,9},{11,1... | collective-permute-start | bytes 1572872 | tf_op jit(solution)/shard_map/ppermute | solution.py:572
  97.4 12.7 %collective-permute-start.27 = (bf16[2,27,16,128]{3,2,1,0:T(8,128)(2,1)S(1)}, bf16[2,27,16,128]{3,2,1,0:T(8,128)(2,1)S(1)}, u32[]{:S(2)}, u32[]{:S(2)}) collective-permute-start(bf16[2,27,16,128]{3,2,1,0:T(8,128)(2,1)S(1)} %get-tuple-element.120), channel_id=1, source_target_pairs={{0,2},{1,3},{2,0},{3,1},{4,6},{5,7},{6,4},{7,5},{8,10},{9,11},{10,... | collective-permute-start | bytes 663560 | tf_op jit(solution)/shard_map/ppermute | solution.py:563
  98.0 14.5 %collective-permute-start.28 = (bf16[4,14,16,128]{3,2,1,0:T(8,128)(2,1)S(1)}, bf16[4,14,16,128]{3,2,1,0:T(8,128)(2,1)S(1)}, u32[]{:S(2)}, u32[]{:S(2)}) collective-permute-start(bf16[4,14,16,128]{3,2,1,0:T(8,128)(2,1)S(1)} %get-tuple-element.123), channel_id=1, source_target_pairs={{0,2},{1,3},{2,0},{3,1},{4,6},{5,7},{6,4},{7,5},{8,10},{9,11},{10,... | collective-permute-start | bytes 688136 | tf_op jit(solution)/shard_map/ppermute | solution.py:563
  99.7 13.8 %collective-permute-start.29 = (bf16[4,13,16,128]{3,2,1,0:T(8,128)(2,1)S(1)}, bf16[4,13,16,128]{3,2,1,0:T(8,128)(2,1)S(1)}, u32[]{:S(2)}, u32[]{:S(2)}) collective-permute-start(bf16[4,13,16,128]{3,2,1,0:T(8,128)(2,1)S(1)} %get-tuple-element.126), channel_id=1, source_target_pairs={{0,4},{1,5},{2,6},{3,7},{4,0},{5,1},{6,2},{7,3},{8,12},{9,13},{10,... | collective-permute-start | bytes 638984 | tf_op jit(solution)/shard_map/ppermute | solution.py:566
  110.1 8.7 %collective-permute-start.30 = (bf16[1,27,16,128]{3,2,1,0:T(8,128)(2,1)S(1)}, bf16[1,27,16,128]{3,2,1,0:T(8,128)(2,1)S(1)}, u32[]{:S(2)}, u32[]{:S(2)}) collective-permute-start(bf16[1,27,16,128]{3,2,1,0:T(8,128)(2,1)S(1)} %get-tuple-element.129), channel_id=1, source_target_pairs={{0,8},{1,9},{2,10},{3,11},{4,12},{5,13},{6,14},{7,15},{8,0},{9,1},... | collective-permute-start | bytes 331784 | tf_op jit(solution)/shard_map/ppermute | solution.py:569
  118.8 8.8 %collective-permute-start.33 = (bf16[1,27,16,128]{3,2,1,0:T(8,128)(2,1)S(1)}, bf16[1,27,16,128]{3,2,1,0:T(8,128)(2,1)S(1)}, u32[]{:S(2)}, u32[]{:S(2)}) collective-permute-start(bf16[1,27,16,128]{3,2,1,0:T(8,128)(2,1)S(1)} %sum_two_zz.1.own), channel_id=1, source_target_pairs={{0,8},{1,9},{2,10},{3,11},{4,12},{5,13},{6,14},{7,15},{8,0},{9,1},... | collective-permute-start | bytes 331784 | tf_op jit(solution)/shard_map/ppermute | solution.py:569
  119.0 9.7 %collective-permute-start.34 = (bf16[1,14,16,128]{3,2,1,0:T(8,128)(2,1)S(1)}, bf16[1,14,16,128]{3,2,1,0:T(8,128)(2,1)S(1)}, u32[]{:S(2)}, u32[]{:S(2)}) collective-permute-start(bf16[1,14,16,128]{3,2,1,0:T(8,128)(2,1)S(1)} %get-tuple-element.138), channel_id=1, source_target_pairs={{0,8},{1,9},{2,10},{3,11},{4,12},{5,13},{6,14},{7,15},{8,0},{9,1},... | collective-permute-start | bytes 172040 | tf_op jit(solution)/shard_map/ppermute | solution.py:569
  136.5 10.6 %collective-permute-start.41 = (bf16[4,27,16,128]{3,2,1,0:T(8,128)(2,1)S(1)}, bf16[4,27,16,128]{3,2,1,0:T(8,128)(2,1)S(1)}, u32[]{:S(2)}, u32[]{:S(2)}) collective-permute-start(bf16[4,27,16,128]{3,2,1,0:T(8,128)(2,1)S(1)} %join_two_z.1.own), channel_id=1, source_target_pairs={{0,2},{1,3},{2,0},{3,1},{4,6},{5,7},{6,4},{7,5},{8,10},{9,11},{10,... | collective-permute-start | bytes 1327112 | tf_op jit(solution)/shard_map/ppermute | solution.py:563
  (31 other events, 170.3 us)

commit v2 on v1

--- a/solution.py
+++ b/solution.py
@@ -426,7 +426,6 @@
     "sum_two_x": 2 * 10**9,
     "sum_a_core": 0,
     "sum_b_core": 0,
-    "first_rim": 3 * 10**9,
     "back_rim": 10**9,
     "sum_a_zz": 2 * 10**9,
     "sum_b_zz": 2 * 10**9,

time: 155 us -> 154 us (level)
  starting transfers between devices: 44.6 us -> 53 us
  local copies, waits for them, and re-layouts: 8.67 us -> 3.85 us
  waiting for transfers between devices: 45.1 us -> 42.3 us
    ppermute x7, waiting for transfers between devices: 9.05 us -> 15.7 us  [to_side(): return lax.ppermute(values, 'dp', [(i, i ^ 2) for i in range(count)])]
    ppermute x6, waiting for transfers between devices: 13.3 us -> 6.78 us  [to_far_level(): return lax.ppermute(values, 'dp', [(i, i ^ 8) for i in range(count)])]
    unnamed x16 -> x8, local copies, waits for them, and re-layouts: 5.61 us -> 1.49 us
    ppermute x10, starting transfers between devices: 18.6 us -> 22.2 us  [rims(): return (lax.ppermute(last, 'dp', ahead), lax.ppermute(first, 'dp', behind))]
    ppermute x7, starting transfers between devices: 5.32 us -> 8.24 us  [to_side(): return lax.ppermute(values, 'dp', [(i, i ^ 2) for i in range(count)])]
    ppermute x5, waiting for transfers between devices: 7.83 us -> 6.05 us  [other(): return lax.ppermute(values, 'chan', [(0, 1), (1, 0)])]
  transfers between devices with their start and end apart: 47 -> 47, of which waited for: 24 -> 25; matrix products, arithmetic and copies ran while one was open for 1% -> 1% of each run, Pallas kernels for 32% -> 31%
where the time goes in v2:
time: 154 us
  Pallas kernels  54 us (35%)
  starting transfers between devices  53 us (34%)
  waiting for transfers between devices  42.3 us (27%)
  local copies, waits for them, and re-layouts  3.85 us (2%)
    pallas_call x10, Pallas kernels, conv_call(): pl.pallas_call(functools.partial(conv_kernel, part, kind, flipped, finish...  40.6 us
    ppermute x10, starting transfers between devices, rims(): return (lax.ppermute(last, 'dp', ahead), lax.ppermute(first, 'dp', behind))  22.2 us
    ppermute x7, waiting for transfers between devices, to_side(): return lax.ppermute(values, 'dp', [(i, i ^ 2) for i in range(count)])  15.7 us
    ppermute x6, starting transfers between devices, to_far_level(): return lax.ppermute(values, 'dp', [(i, i ^ 8) for i in range(count)])  8.98 us
    ppermute x7, starting transfers between devices, to_side(): return lax.ppermute(values, 'dp', [(i, i ^ 2) for i in range(count)])  8.24 us
    pallas_call x2, Pallas kernels, filter_call(): pl.pallas_call(functools.partial(filter_kernel, colours), grid=(1,), out_...  7.88 us
    ppermute x5, starting transfers between devices, other(): return lax.ppermute(values, 'chan', [(0, 1), (1, 0)])  7.78 us
    ppermute x6, waiting for transfers between devices, to_far_level(): return lax.ppermute(values, 'dp', [(i, i ^ 8) for i in range(count)])  6.78 us
  transfers between devices with their start and end apart: 47, of which 25 were waited for; matrix products, arithmetic and copies ran while one was open for 1% of the time, Pallas kernels for 31%

profile of v2, /device:TPU:0, one launch (start us, length us, event | category | flops | bytes accessed | tf_op | source)
XLA Modules:
  0.0 154.1 jit_solution(1726931288229292028)
XLA Ops:
  1.9 3.0 %collective-permute-start = (bf16[27,32,256]{2,1,0:T(8,128)(2,1)S(1)}, bf16[27,32,256]{2,1,0:T(8,128)(2,1)}, u32[]{:S(2)}, u32[]{:S(2)}) collective-permute-start(bf16[27,32,256]{2,1,0:T(8,128)(2,1)S(1)} %constant_dynamic-slice_fusion.2), channel_id=1, source_target_pairs={{0,16},{16,0},{1,17},{17,1},{2,18},{18,2},{3,19},{19,3},{4,20},{20... | collective-permute-start | bytes 1327112 | tf_op jit(solution)/shard_map/ppermute | solution.py:556
  6.1 4.4 %collective-permute-start.2 = (bf16[1,32,32,128]{3,2,1,0:T(8,128)(2,1)S(1)}, bf16[1,32,32,128]{3,2,1,0:T(8,128)(2,1)S(1)}, u32[]{:S(2)}, u32[]{:S(2)}) collective-permute-start(bf16[1,32,32,128]{3,2,1,0:T(8,128)(2,1)S(1)} %get-tuple-element.156), channel_id=1, source_target_pairs={{1,0},{2,1},{3,2},{4,3},{5,4},{6,5},{7,6},{8,7},{9,8},{10,9},{11,1... | collective-permute-start | bytes 786440 | tf_op jit(solution)/shard_map/ppermute | solution.py:571
  10.5 4.2 %collective-permute-done.1.refs_0_ = bf16[1,32,32,128]{3,2,1,0:T(8,128)(2,1)S(1)} collective-permute-done((bf16[1,32,32,128]{3,2,1,0:T(8,128)(2,1)S(1)}, bf16[1,32,32,128]{3,2,1,0:T(8,128)(2,1)S(1)}, u32[]{:S(2)}, u32[]{:S(2)}) %collective-permute-start.1) | collective-permute-done | bytes 262176 | tf_op jit(solution)/shard_map/ppermute | solution.py:571
  20.0 5.4 %first_own.1 = (f32[2,32,32,256]{3,2,1,0:T(8,128)S(1)}, bf16[27,128,256]{2,1,0:T(8,128)(2,1)S(1)}) custom-call(bf16[1,32,32,128]{3,2,1,0:T(8,128)(2,1)S(1)} %collective-permute-done.1.refs_0_, bf16[2,32,32,128]{3,2,1,0:T(8,128)(2,1)S(1)} %copy-done.1, bf16[1,32,32,128]{3,2,1,0:T(8,128)(2,1)S(1)} %collective-permute-done.2.refs_2_.refs_3_, ...), custom_call_target="tpu_custom_call" | custom-call | tf_op jit(solution)/shard_map/first_own/pallas_call | solution.py:503
  25.4 3.8 %collective-permute-done.6.refs_2_ = bf16[27,32,256]{2,1,0:T(8,128)(2,1)} collective-permute-done((bf16[27,32,256]{2,1,0:T(8,128)(2,1)}, bf16[27,32,256]{2,1,0:T(8,128)(2,1)}, u32[]{:S(2)}, u32[]{:S(2)}) %collective-permute-start.6) | collective-permute-done | bytes 442400 | tf_op jit(solution)/shard_map/ppermute | solution.py:562
  32.3 4.4 %collective-permute-start.5 = (bf16[1,32,32,128]{3,2,1,0:T(8,128)(2,1)S(1)}, bf16[1,32,32,128]{3,2,1,0:T(8,128)(2,1)S(1)}, u32[]{:S(2)}, u32[]{:S(2)}) collective-permute-start(bf16[1,32,32,128]{3,2,1,0:T(8,128)(2,1)S(1)} %get-tuple-element.154), channel_id=1, source_target_pairs={{1,0},{2,1},{3,2},{4,3},{5,4},{6,5},{7,6},{8,7},{9,8},{10,9},{11,1... | collective-permute-start | bytes 786440 | tf_op jit(solution)/shard_map/ppermute | solution.py:571
  36.7 4.2 %first_other.1 = (f32[2,32,32,256]{3,2,1,0:T(8,128)S(1)}, bf16[27,128,256]{2,1,0:T(8,128)(2,1)S(1)}) custom-call(bf16[2,32,32,128]{3,2,1,0:T(8,128)(2,1)S(1)} %collective-permute-done.3.refs_0_, bf16[27,32,256]{2,1,0:T(8,128)(2,1)} %collective-permute-done.refs_1_, bf16[27,32,256]{2,1,0:T(8,128)(2,1)} %collective-permute-done.6.refs_2_, ...), custom_call_target="tpu_custom_call" | custom-call | tf_op jit(solution)/shard_map/first_other/pallas_call | solution.py:503
  42.8 4.3 %collective-permute-start.10 = (bf16[1,32,32,256]{3,2,1,0:T(8,128)(2,1)S(1)}, bf16[1,32,32,256]{3,2,1,0:T(8,128)(2,1)S(1)}, u32[]{:S(2)}, u32[]{:S(2)}) collective-permute-start(bf16[1,32,32,256]{3,2,1,0:T(8,128)(2,1)S(1)} %get-tuple-element.85.refs_0_.refs_1_.refs_4_), channel_id=1, source_target_pairs={{1,0},{2,1},{3,2},{4,3},{5,4},{6,5},{7,6},{8,7},{9,8},{10,9},{11,1... | collective-permute-start | bytes 1572872 | tf_op jit(solution)/shard_map/ppermute | solution.py:571
  48.1 4.2 %second_own.1 = (f32[2,32,32,256]{3,2,1,0:T(8,128)S(1)}, bf16[27,128,256]{2,1,0:T(8,128)(2,1)}) custom-call(bf16[1,32,32,256]{3,2,1,0:T(8,128)(2,1)S(1)} %get-tuple-element.85.refs_0_.refs_1_.refs_4_, bf16[1,32,32,256]{3,2,1,0:T(8,128)(2,1)S(1)} %get-tuple-element.84.refs_1_.refs_2_.refs_5_, bf16[27,128,256]{2,1,0:T(8,128)(2,1)S(1)} %bitcast.5), custom_call_target="tpu_custom_call" | custom-call | tf_op jit(solution)/shard_map/second_own/pallas_call | solution.py:503
  54.8 3.8 %second_other.1 = (f32[2,32,32,256]{3,2,1,0:T(8,128)S(1)}, bf16[27,256,256]{2,1,0:T(8,128)(2,1)S(1)}) custom-call(bf16[1,32,32,256]{3,2,1,0:T(8,128)(2,1)S(1)} %get-tuple-element.85.refs_0_.refs_1_.refs_4_, bf16[1,32,32,256]{3,2,1,0:T(8,128)(2,1)S(1)} %get-tuple-element.84.refs_1_.refs_2_.refs_5_, bf16[27,128,256]{2,1,0:T(8,128)(2,1)S(1)} %bitcast.6, ...), custom_call_target="tpu_custom_call" | custom-call | tf_op jit(solution)/shard_map/second_other/pallas_call | solution.py:503
  58.6 4.4 %collective-permute-done.15.refs_5_ = bf16[2,32,32,128]{3,2,1,0:T(8,128)(2,1)S(1)} collective-permute-done((bf16[2,32,32,128]{3,2,1,0:T(8,128)(2,1)S(1)}, bf16[2,32,32,128]{3,2,1,0:T(8,128)(2,1)S(1)}, u32[]{:S(2)}, u32[]{:S(2)}) %collective-permute-start.15) | collective-permute-done | bytes 524320 | tf_op jit(solution)/shard_map/ppermute | solution.py:556
  63.0 3.6 %second_rim.1 = (bf16[2,32,32,128]{3,2,1,0:T(8,128)(2,1)}, bf16[1,32,32,256]{3,2,1,0:T(8,128)(2,1)S(1)}, bf16[1,32,32,256]{3,2,1,0:T(8,128)(2,1)S(1)}) custom-call(bf16[1,32,32,256]{3,2,1,0:T(8,128)(2,1)S(1)} %collective-permute-done.9.refs_0_, bf16[1,32,32,256]{3,2,1,0:T(8,128)(2,1)S(1)} %collective-permute-done.10.refs_1_.refs_3_, ...), custom_call_target="tpu_custom_call" | custom-call | tf_op jit(solution)/shard_map/second_rim/pallas_call | solution.py:503
  66.6 4.4 %collective-permute-start.17 = (bf16[1,32,32,256]{3,2,1,0:T(8,128)(2,1)S(1)}, bf16[1,32,32,256]{3,2,1,0:T(8,128)(2,1)S(1)}, u32[]{:S(2)}, u32[]{:S(2)}) collective-permute-start(bf16[1,32,32,256]{3,2,1,0:T(8,128)(2,1)S(1)} %get-tuple-element.96.refs_4_.refs_0_), channel_id=1, source_target_pairs={{1,0},{2,1},{3,2},{4,3},{5,4},{6,5},{7,6},{8,7},{9,8},{10,9},{11,1... | collective-permute-start | bytes 1572872 | tf_op jit(solution)/shard_map/ppermute | solution.py:571
  71.0 4.0 %grad_two.1 = (f32[8,27,16,128]{3,2,1,0:T(8,128)S(1)}, bf16[4,27,16,128]{3,2,1,0:T(8,128)(2,1)S(1)}, bf16[4,27,16,128]{3,2,1,0:T(8,128)(2,1)S(1)}) custom-call(bf16[1,32,32,256]{3,2,1,0:T(8,128)(2,1)S(1)} %collective-permute-done.9.refs_0_, bf16[1,32,32,256]{3,2,1,0:T(8,128)(2,1)S(1)} %get-tuple-element.85.refs_0_.refs_1_.refs_4_, ...), custom_call_target="tpu_custom_call" | custom-call | tf_op jit(solution)/shard_map/grad_two/pallas_call | solution.py:525
  77.8 5.4 %back_local.1.refs_3_ = f32[2,32,32,256]{3,2,1,0:T(8,128)S(1)} custom-call(bf16[1,32,32,256]{3,2,1,0:T(8,128)(2,1)S(1)} %get-tuple-element.96.refs_4_.refs_0_, bf16[1,32,32,256]{3,2,1,0:T(8,128)(2,1)S(1)} %get-tuple-element.101.refs_5_.refs_1_, bf16[27,256,256]{2,1,0:T(8,128)(2,1)S(1)} %get-tuple-element.91.refs_2_), custom_call_target="tpu_custom_call" | custom-call | tf_op jit(solution)/shard_map/back_local/pallas_call | solution.py:503
  83.3 2.8 %back_rim.1 = (bf16[1,32,32,256]{3,2,1,0:T(8,128)(2,1)S(1)}, bf16[1,32,32,256]{3,2,1,0:T(8,128)(2,1)S(1)}) custom-call(bf16[1,32,32,256]{3,2,1,0:T(8,128)(2,1)S(1)} %collective-permute-done.16.refs_0_, bf16[1,32,32,256]{3,2,1,0:T(8,128)(2,1)S(1)} %collective-permute-done.17.refs_1_, bf16[27,256,256]{2,1,0:T(8,128)(2,1)S(1)} %get-tuple-element.91.refs_2_, ...), custom_call_target="tpu_custom_call" | custom-call | flops 1000000000 | tf_op jit(solution)/shard_map/back_rim/pallas_call | solution.py:503
  86.2 4.3 %collective-permute-start.26 = (bf16[1,32,32,256]{3,2,1,0:T(8,128)(2,1)S(1)}, bf16[1,32,32,256]{3,2,1,0:T(8,128)(2,1)S(1)}, u32[]{:S(2)}, u32[]{:S(2)}) collective-permute-start(bf16[1,32,32,256]{3,2,1,0:T(8,128)(2,1)S(1)} %get-tuple-element.117.refs_4_.refs_0_), channel_id=1, source_target_pairs={{1,0},{2,1},{3,2},{4,3},{5,4},{6,5},{7,6},{8,7},{9,8},{10,9},{11,1... | collective-permute-start | bytes 1572872 | tf_op jit(solution)/shard_map/ppermute | solution.py:571
  90.5 3.9 %grad_one.1 = (f32[8,14,16,128]{3,2,1,0:T(8,128)S(1)}, bf16[4,14,16,128]{3,2,1,0:T(8,128)(2,1)S(1)}, bf16[4,14,16,128]{3,2,1,0:T(8,128)(2,1)S(1)}, f32[8,13,16,1...) custom-call(bf16[1,32,32,128]{3,2,1,0:T(8,128)(2,1)S(1)} %collective-permute-done.1.ref, ...), custom_call_target="tpu_custom_call" | custom-call | tf_op jit(solution)/shard_map/grad_one/pallas_call | solution.py:525
  98.6 5.9 %first_back_local.1.refs_3_ = f32[2,32,32,128]{3,2,1,0:T(8,128)S(1)} custom-call(bf16[1,32,32,256]{3,2,1,0:T(8,128)(2,1)S(1)} %get-tuple-element.117.refs_4_.refs_0_, bf16[1,32,32,256]{3,2,1,0:T(8,128)(2,1)S(1)} %get-tuple-element.102.refs_5_.refs_1_, bf16[27,128,256]{2,1,0:T(8,128)(2,1)S(1)} %get-tuple-element.118.refs_2_), custom_call_target="tpu_custom_call" | custom-call | tf_op jit(solution)/shard_map/first_back_local/pallas_call | solution.py:503
  104.6 2.8 %collective-permute-done.27.came = bf16[2,27,16,128]{3,2,1,0:T(8,128)(2,1)S(1)} collective-permute-done((bf16[2,27,16,128]{3,2,1,0:T(8,128)(2,1)S(1)}, bf16[2,27,16,128]{3,2,1,0:T(8,128)(2,1)S(1)}, u32[]{:S(2)}, u32[]{:S(2)}) %collective-permute-start.27) | collective-permute-done | bytes 221216 | tf_op jit(solution)/shard_map/ppermute | solution.py:562
  126.7 3.4 %collective-permute-done.36.came = bf16[2,27,16,128]{3,2,1,0:T(8,128)(2,1)S(1)} collective-permute-done((bf16[2,27,16,128]{3,2,1,0:T(8,128)(2,1)S(1)}, bf16[2,27,16,128]{3,2,1,0:T(8,128)(2,1)S(1)}, u32[]{:S(2)}, u32[]{:S(2)}) %collective-permute-start.36) | collective-permute-done | bytes 221216 | tf_op jit(solution)/shard_map/ppermute | solution.py:565
  135.0 2.8 %collective-permute-start.42 = (bf16[4,14,16,128]{3,2,1,0:T(8,128)(2,1)S(1)}, bf16[4,14,16,128]{3,2,1,0:T(8,128)(2,1)S(1)}, u32[]{:S(2)}, u32[]{:S(2)}) collective-permute-start(bf16[4,14,16,128]{3,2,1,0:T(8,128)(2,1)S(1)} %join_a_z.1.own), channel_id=1, source_target_pairs={{0,2},{1,3},{2,0},{3,1},{4,6},{5,7},{6,4},{7,5},{8,10},{9,11},{10,... | collective-permute-start | bytes 688136 | tf_op jit(solution)/shard_map/ppermute | solution.py:562
  138.9 3.4 %first_back_rim.1 = bf16[2,32,32,128]{3,2,1,0:T(8,128)(2,1)} custom-call(bf16[1,32,32,256]{3,2,1,0:T(8,128)(2,1)S(1)} %collective-permute-done.20.refs_0_, bf16[1,32,32,256]{3,2,1,0:T(8,128)(2,1)S(1)} %collective-permute-done.26.refs_1_, bf16[27,128,256]{2,1,0:T(8,128)(2,1)S(1)} %get-tuple-element.118.refs_2_, f32[2,32,32,128]{3,2,1,0:T(8,128)S(1)} %first_back_local.1.refs_3_), custom_call_target="tpu_custom_call" | custom-call | tf_op jit(solution)/shard_map/first_back_rim/pallas_call | solution.py:503
  142.3 4.2 %collective-permute-done.41.came = bf16[4,27,16,128]{3,2,1,0:T(8,128)(2,1)S(1)} collective-permute-done((bf16[4,27,16,128]{3,2,1,0:T(8,128)(2,1)S(1)}, bf16[4,27,16,128]{3,2,1,0:T(8,128)(2,1)S(1)}, u32[]{:S(2)}, u32[]{:S(2)}) %collective-permute-start.41) | collective-permute-done | bytes 442400 | tf_op jit(solution)/shard_map/ppermute | solution.py:562
  (117 shorter events, 56.0 us)
Async XLA Ops:
  1.9 13.3 %collective-permute-start = (bf16[27,32,256]{2,1,0:T(8,128)(2,1)S(1)}, bf16[27,32,256]{2,1,0:T(8,128)(2,1)}, u32[]{:S(2)}, u32[]{:S(2)}) collective-permute-start(bf16[27,32,256]{2,1,0:T(8,128)(2,1)S(1)} %constant_dynamic-slice_fusion.2), channel_id=1, source_target_pairs={{0,16},{16,0},{1,17},{17,1},{2,18},{18,2},{3,19},{19,3},{4,20},{20... | collective-permute-start | bytes 1327112 | tf_op jit(solution)/shard_map/ppermute | solution.py:556
  6.0 8.7 %collective-permute-start.1 = (bf16[1,32,32,128]{3,2,1,0:T(8,128)(2,1)S(1)}, bf16[1,32,32,128]{3,2,1,0:T(8,128)(2,1)S(1)}, u32[]{:S(2)}, u32[]{:S(2)}) collective-permute-start(bf16[1,32,32,128]{3,2,1,0:T(8,128)(2,1)S(1)} %get-tuple-element.157), channel_id=1, source_target_pairs={{0,1},{1,2},{2,3},{3,4},{4,5},{5,6},{6,7},{7,8},{8,9},{9,10},{10,1... | collective-permute-start | bytes 786440 | tf_op jit(solution)/shard_map/ppermute | solution.py:571
  15.2 14.9 %collective-permute-start.3 = (bf16[2,32,32,128]{3,2,1,0:T(8,128)(2,1)}, bf16[2,32,32,128]{3,2,1,0:T(8,128)(2,1)S(1)}, u32[]{:S(2)}, u32[]{:S(2)}) collective-permute-start(bf16[2,32,32,128]{3,2,1,0:T(8,128)(2,1)} %refs_2_.1), channel_id=1, source_target_pairs={{0,16},{16,0},{1,17},{17,1},{2,18},{18,2},{3,19},{19,3},{4,20},{20... | collective-permute-start | bytes 1572872 | tf_op jit(solution)/shard_map/ppermute | solution.py:556
  16.9 12.2 %collective-permute-start.6 = (bf16[27,32,256]{2,1,0:T(8,128)(2,1)}, bf16[27,32,256]{2,1,0:T(8,128)(2,1)}, u32[]{:S(2)}, u32[]{:S(2)}) collective-permute-start(bf16[27,32,256]{2,1,0:T(8,128)(2,1)} %collective-permute-done.refs_1_), channel_id=1, source_target_pairs={{0,2},{1,3},{2,0},{3,1},{4,6},{5,7},{6,4},{7,5},{8,10},{9,11},{10,... | collective-permute-start | bytes 1327112 | tf_op jit(solution)/shard_map/ppermute | solution.py:562
  18.4 13.8 %collective-permute-start.7 = (bf16[27,32,256]{2,1,0:T(8,128)(2,1)}, bf16[27,32,256]{2,1,0:T(8,128)(2,1)}, u32[]{:S(2)}, u32[]{:S(2)}) collective-permute-start(bf16[27,32,256]{2,1,0:T(8,128)(2,1)} %collective-permute-done.refs_1_), channel_id=1, source_target_pairs={{0,1},{1,0},{2,3},{3,2},{4,5},{5,4},{6,7},{7,6},{8,9},{9,8},{10,11... | collective-permute-start | bytes 1327112 | tf_op jit(solution)/shard_map/ppermute | solution.py:559
  30.1 22.2 %collective-permute-start.12 = (bf16[27,32,256]{2,1,0:T(8,128)(2,1)S(1)}, bf16[27,32,256]{2,1,0:T(8,128)(2,1)S(1)}, u32[]{:S(2)}, u32[]{:S(2)}) collective-permute-start(bf16[27,32,256]{2,1,0:T(8,128)(2,1)S(1)} %get-tuple-element.89), channel_id=1, source_target_pairs={{0,16},{16,0},{1,17},{17,1},{2,18},{18,2},{3,19},{19,3},{4,20},{20... | collective-permute-start | bytes 1327112 | tf_op jit(solution)/shard_map/ppermute | solution.py:556
  31.1 21.5 %collective-permute-start.11 = (bf16[27,32,256]{2,1,0:T(8,128)(2,1)S(1)}, bf16[27,32,256]{2,1,0:T(8,128)(2,1)S(1)}, u32[]{:S(2)}, u32[]{:S(2)}) collective-permute-start(bf16[27,32,256]{2,1,0:T(8,128)(2,1)S(1)} %get-tuple-element.86), channel_id=1, source_target_pairs={{0,16},{16,0},{1,17},{17,1},{2,18},{18,2},{3,19},{19,3},{4,20},{20... | collective-permute-start | bytes 1327112 | tf_op jit(solution)/shard_map/ppermute | solution.py:556
  32.2 8.7 %collective-permute-start.4 = (bf16[1,32,32,128]{3,2,1,0:T(8,128)(2,1)S(1)}, bf16[1,32,32,128]{3,2,1,0:T(8,128)(2,1)S(1)}, u32[]{:S(2)}, u32[]{:S(2)}) collective-permute-start(bf16[1,32,32,128]{3,2,1,0:T(8,128)(2,1)S(1)} %get-tuple-element.155), channel_id=1, source_target_pairs={{0,1},{1,2},{2,3},{3,4},{4,5},{5,6},{6,7},{7,8},{8,9},{9,10},{10,1... | collective-permute-start | bytes 786440 | tf_op jit(solution)/shard_map/ppermute | solution.py:571
  32.3 8.6 %collective-permute-start.5 = (bf16[1,32,32,128]{3,2,1,0:T(8,128)(2,1)S(1)}, bf16[1,32,32,128]{3,2,1,0:T(8,128)(2,1)S(1)}, u32[]{:S(2)}, u32[]{:S(2)}) collective-permute-start(bf16[1,32,32,128]{3,2,1,0:T(8,128)(2,1)S(1)} %get-tuple-element.154), channel_id=1, source_target_pairs={{1,0},{2,1},{3,2},{4,3},{5,4},{6,5},{7,6},{8,7},{9,8},{10,9},{11,1... | collective-permute-start | bytes 786440 | tf_op jit(solution)/shard_map/ppermute | solution.py:571
  42.8 20.2 %collective-permute-start.10 = (bf16[1,32,32,256]{3,2,1,0:T(8,128)(2,1)S(1)}, bf16[1,32,32,256]{3,2,1,0:T(8,128)(2,1)S(1)}, u32[]{:S(2)}, u32[]{:S(2)}) collective-permute-start(bf16[1,32,32,256]{3,2,1,0:T(8,128)(2,1)S(1)} %get-tuple-element.85.refs_0_.refs_1_.refs_4_), channel_id=1, source_target_pairs={{1,0},{2,1},{3,2},{4,3},{5,4},{6,5},{7,6},{8,7},{9,8},{10,9},{11,1... | collective-permute-start | bytes 1572872 | tf_op jit(solution)/shard_map/ppermute | solution.py:571
  47.1 15.9 %collective-permute-start.15 = (bf16[2,32,32,128]{3,2,1,0:T(8,128)(2,1)S(1)}, bf16[2,32,32,128]{3,2,1,0:T(8,128)(2,1)S(1)}, u32[]{:S(2)}, u32[]{:S(2)}) collective-permute-start(bf16[2,32,32,128]{3,2,1,0:T(8,128)(2,1)S(1)} %copy-done.3), channel_id=1, source_target_pairs={{0,16},{16,0},{1,17},{17,1},{2,18},{18,2},{3,19},{19,3},{4,20},{20... | collective-permute-start | bytes 1572872 | tf_op jit(solution)/shard_map/ppermute | solution.py:556
  48.1 14.9 %collective-permute-start.9 = (bf16[1,32,32,256]{3,2,1,0:T(8,128)(2,1)S(1)}, bf16[1,32,32,256]{3,2,1,0:T(8,128)(2,1)S(1)}, u32[]{:S(2)}, u32[]{:S(2)}) collective-permute-start(bf16[1,32,32,256]{3,2,1,0:T(8,128)(2,1)S(1)} %get-tuple-element.84.refs_1_.refs_2_.refs_5_), channel_id=1, source_target_pairs={{0,1},{1,2},{2,3},{3,4},{4,5},{5,6},{6,7},{7,8},{8,9},{9,10},{10,1... | collective-permute-start | bytes 1572872 | tf_op jit(solution)/shard_map/ppermute | solution.py:571
  66.6 16.7 %collective-permute-start.16 = (bf16[1,32,32,256]{3,2,1,0:T(8,128)(2,1)S(1)}, bf16[1,32,32,256]{3,2,1,0:T(8,128)(2,1)S(1)}, u32[]{:S(2)}, u32[]{:S(2)}) collective-permute-start(bf16[1,32,32,256]{3,2,1,0:T(8,128)(2,1)S(1)} %get-tuple-element.101.refs_5_.refs_1_), channel_id=1, source_target_pairs={{0,1},{1,2},{2,3},{3,4},{4,5},{5,6},{6,7},{7,8},{8,9},{9,10},{10,1... | collective-permute-start | bytes 1572872 | tf_op jit(solution)/shard_map/ppermute | solution.py:571
  66.6 16.7 %collective-permute-start.17 = (bf16[1,32,32,256]{3,2,1,0:T(8,128)(2,1)S(1)}, bf16[1,32,32,256]{3,2,1,0:T(8,128)(2,1)S(1)}, u32[]{:S(2)}, u32[]{:S(2)}) collective-permute-start(bf16[1,32,32,256]{3,2,1,0:T(8,128)(2,1)S(1)} %get-tuple-element.96.refs_4_.refs_0_), channel_id=1, source_target_pairs={{1,0},{2,1},{3,2},{4,3},{5,4},{6,5},{7,6},{8,7},{9,8},{10,9},{11,1... | collective-permute-start | bytes 1572872 | tf_op jit(solution)/shard_map/ppermute | solution.py:571
  77.7 17.3 %collective-permute-start.21 = (bf16[4,27,16,128]{3,2,1,0:T(8,128)(2,1)S(1)}, bf16[4,27,16,128]{3,2,1,0:T(8,128)(2,1)S(1)}, u32[]{:S(2)}, u32[]{:S(2)}) collective-permute-start(bf16[4,27,16,128]{3,2,1,0:T(8,128)(2,1)S(1)} %get-tuple-element.107), channel_id=1, source_target_pairs={{0,4},{1,5},{2,6},{3,7},{4,0},{5,1},{6,2},{7,3},{8,12},{9,13},{10,... | collective-permute-start | bytes 1327112 | tf_op jit(solution)/shard_map/ppermute | solution.py:565
  86.0 18.5 %collective-permute-start.20 = (bf16[1,32,32,256]{3,2,1,0:T(8,128)(2,1)S(1)}, bf16[1,32,32,256]{3,2,1,0:T(8,128)(2,1)S(1)}, u32[]{:S(2)}, u32[]{:S(2)}) collective-permute-start(bf16[1,32,32,256]{3,2,1,0:T(8,128)(2,1)S(1)} %get-tuple-element.102.refs_5_.refs_1_), channel_id=1, source_target_pairs={{0,1},{1,2},{2,3},{3,4},{4,5},{5,6},{6,7},{7,8},{8,9},{9,10},{10,1... | collective-permute-start | bytes 1572872 | tf_op jit(solution)/shard_map/ppermute | solution.py:571
  86.2 18.3 %collective-permute-start.26 = (bf16[1,32,32,256]{3,2,1,0:T(8,128)(2,1)S(1)}, bf16[1,32,32,256]{3,2,1,0:T(8,128)(2,1)S(1)}, u32[]{:S(2)}, u32[]{:S(2)}) collective-permute-start(bf16[1,32,32,256]{3,2,1,0:T(8,128)(2,1)S(1)} %get-tuple-element.117.refs_4_.refs_0_), channel_id=1, source_target_pairs={{1,0},{2,1},{3,2},{4,3},{5,4},{6,5},{7,6},{8,7},{9,8},{10,9},{11,1... | collective-permute-start | bytes 1572872 | tf_op jit(solution)/shard_map/ppermute | solution.py:571
  96.0 11.4 %collective-permute-start.27 = (bf16[2,27,16,128]{3,2,1,0:T(8,128)(2,1)S(1)}, bf16[2,27,16,128]{3,2,1,0:T(8,128)(2,1)S(1)}, u32[]{:S(2)}, u32[]{:S(2)}) collective-permute-start(bf16[2,27,16,128]{3,2,1,0:T(8,128)(2,1)S(1)} %get-tuple-element.120), channel_id=1, source_target_pairs={{0,2},{1,3},{2,0},{3,1},{4,6},{5,7},{6,4},{7,5},{8,10},{9,11},{10,... | collective-permute-start | bytes 663560 | tf_op jit(solution)/shard_map/ppermute | solution.py:562
  96.6 13.7 %collective-permute-start.28 = (bf16[4,14,16,128]{3,2,1,0:T(8,128)(2,1)S(1)}, bf16[4,14,16,128]{3,2,1,0:T(8,128)(2,1)S(1)}, u32[]{:S(2)}, u32[]{:S(2)}) collective-permute-start(bf16[4,14,16,128]{3,2,1,0:T(8,128)(2,1)S(1)} %get-tuple-element.123), channel_id=1, source_target_pairs={{0,2},{1,3},{2,0},{3,1},{4,6},{5,7},{6,4},{7,5},{8,10},{9,11},{10,... | collective-permute-start | bytes 688136 | tf_op jit(solution)/shard_map/ppermute | solution.py:562
  98.3 13.9 %collective-permute-start.29 = (bf16[4,13,16,128]{3,2,1,0:T(8,128)(2,1)S(1)}, bf16[4,13,16,128]{3,2,1,0:T(8,128)(2,1)S(1)}, u32[]{:S(2)}, u32[]{:S(2)}) collective-permute-start(bf16[4,13,16,128]{3,2,1,0:T(8,128)(2,1)S(1)} %get-tuple-element.126), channel_id=1, source_target_pairs={{0,4},{1,5},{2,6},{3,7},{4,0},{5,1},{6,2},{7,3},{8,12},{9,13},{10,... | collective-permute-start | bytes 638984 | tf_op jit(solution)/shard_map/ppermute | solution.py:565
  113.3 8.8 %collective-permute-start.33 = (bf16[1,27,16,128]{3,2,1,0:T(8,128)(2,1)S(1)}, bf16[1,27,16,128]{3,2,1,0:T(8,128)(2,1)S(1)}, u32[]{:S(2)}, u32[]{:S(2)}) collective-permute-start(bf16[1,27,16,128]{3,2,1,0:T(8,128)(2,1)S(1)} %sum_two_zz.1.own), channel_id=1, source_target_pairs={{0,8},{1,9},{2,10},{3,11},{4,12},{5,13},{6,14},{7,15},{8,0},{9,1},... | collective-permute-start | bytes 331784 | tf_op jit(solution)/shard_map/ppermute | solution.py:568
  133.8 12.8 %collective-permute-start.41 = (bf16[4,27,16,128]{3,2,1,0:T(8,128)(2,1)S(1)}, bf16[4,27,16,128]{3,2,1,0:T(8,128)(2,1)S(1)}, u32[]{:S(2)}, u32[]{:S(2)}) collective-permute-start(bf16[4,27,16,128]{3,2,1,0:T(8,128)(2,1)S(1)} %join_two_z.1.own), channel_id=1, source_target_pairs={{0,2},{1,3},{2,0},{3,1},{4,6},{5,7},{6,4},{7,5},{8,10},{9,11},{10,... | collective-permute-start | bytes 1327112 | tf_op jit(solution)/shard_map/ppermute | solution.py:562
  135.0 14.0 %collective-permute-start.42 = (bf16[4,14,16,128]{3,2,1,0:T(8,128)(2,1)S(1)}, bf16[4,14,16,128]{3,2,1,0:T(8,128)(2,1)S(1)}, u32[]{:S(2)}, u32[]{:S(2)}) collective-permute-start(bf16[4,14,16,128]{3,2,1,0:T(8,128)(2,1)S(1)} %join_a_z.1.own), channel_id=1, source_target_pairs={{0,2},{1,3},{2,0},{3,1},{4,6},{5,7},{6,4},{7,5},{8,10},{9,11},{10,... | collective-permute-start | bytes 688136 | tf_op jit(solution)/shard_map/ppermute | solution.py:562
  137.9 11.3 %collective-permute-start.43 = (bf16[4,13,16,128]{3,2,1,0:T(8,128)(2,1)S(1)}, bf16[4,13,16,128]{3,2,1,0:T(8,128)(2,1)S(1)}, u32[]{:S(2)}, u32[]{:S(2)}) collective-permute-start(bf16[4,13,16,128]{3,2,1,0:T(8,128)(2,1)S(1)} %join_b_x.1.own), channel_id=1, source_target_pairs={{0,4},{1,5},{2,6},{3,7},{4,0},{5,1},{6,2},{7,3},{8,12},{9,13},{10,... | collective-permute-start | bytes 638984 | tf_op jit(solution)/shard_map/ppermute | solution.py:565
  (27 other events, 145.0 us)
